TPU v7x, 512 devices: a whole 4x8x8 slice. The times are simulated.
512 devices in a mesh: seq: 16 (over z, core), exp: 32 (over y, x).
Axes of the slice: x: 4, y: 8, z: 8, core: 2. Of those that a mesh axis runs over, the one named last changes fastest.
Arguments:
- tokens: bfloat16 [32, 4096, 768], P('exp', 'seq'), may hold values from -6 to 6
- w_in: bfloat16 [768, 3072], P('seq'), may hold values from -0.21875 to 0.21875
- w_small: bfloat16 [768, 56], replicated, may hold values from -0.21875 to 0.21875
- dt_bias: float32 [24], replicated, may hold values from -1 to 1
- decay_rate: float32 [24], replicated, may hold values from 4.8828125e-05 to 0.08, as said below
- conv_w: float32 [4, 1536], replicated, may hold values from -3 to 3
- conv_b: float32 [1536], replicated, may hold values from -3 to 3
- skip: float32 [24], replicated, may hold values from 0.5 to 1.5
- norm_gain: float32 [1536], replicated, may hold values from 0.1 to 1.9
- w_out: bfloat16 [1536, 768], P('seq'), may hold values from -0.15625 to 0.15625
- w_router: bfloat16 [768, 32], replicated, may hold values from -0.21875 to 0.21875
- expert_ids: int32 [32, 4096, 2], P('exp', 'seq'), may hold values from 0 to 31, all different within a row; in each aligned block of 256 rows (0 to 255, 256 to 511, ..., all dimensions but the last counted through in order) at most 48 rows name the same one
- w_gate: bfloat16 [32, 768, 768], P('exp'), may hold values from -0.21875 to 0.21875
- w_up: bfloat16 [32, 768, 768], P('exp'), may hold values from -0.21875 to 0.21875
- w_down: bfloat16 [32, 768, 768], P('exp'), may hold values from -0.21875 to 0.21875
Outputs:
- out: bfloat16 [32, 4096, 768], P('exp', 'seq')
Inputs may be any that keep to these rules, and one draw needn't show every extreme that they name: `expert_ids`: in the rows of one device no expert is named by more than 48 tokens, a bound that some block reaches; the two experts of a token differ. `decay_rate`: positive rates, one per head.
All inputs are finite; a program needn't handle non-finite values.
Results may differ from a plain program's by a relative error of at most 0.015.
Values may be sent and summed in bfloat16 or wider, within the bound.
A program may use at most 64 MiB of HBM per device.

v0:
```python
import jax
import jax.numpy as jnp
from jax import lax
from jax.sharding import PartitionSpec as P

SCAN_BLOCK = 128


EPSILON = 1e-05
HIGHEST = lax.Precision.HIGHEST


def from_behind(block, axis, distance):
    devices = range(lax.axis_size(axis))
    route = [(i - distance, i) for i in devices if i - distance in devices]
    return lax.ppermute(block, axis, route)


def carried_in(part, axis, combine, identity):
    place = lax.axis_index(axis)
    gathered = jax.tree.map(lambda a: lax.all_gather(a, axis), part)
    state = jax.tree.map(lambda a, e: jnp.zeros_like(a) + jnp.asarray(e, a.dtype), part, identity)

    def one(lap, state):
        return combine(
            state, jax.tree.map(lambda a: lax.dynamic_index_in_dim(a, lap, 0, False), gathered)
        )

    return lax.fori_loop(0, place, one, state)


def rms_rows(values):
    return values * lax.rsqrt(jnp.mean(values * values, axis=-1, keepdims=True) + EPSILON)


def expert_block(rows_in, gate_mat, up_mat, down_mat):
    hidden = jax.nn.silu(jnp.dot(rows_in, gate_mat, preferred_element_type=jnp.float32)) * jnp.dot(
        rows_in, up_mat, preferred_element_type=jnp.float32
    )
    return jnp.dot(
        hidden.astype(jnp.bfloat16), down_mat, preferred_element_type=jnp.float32
    ).astype(jnp.bfloat16)


def local(
    tokens,
    w_in,
    w_small,
    dt_bias,
    decay_rate,
    conv_w,
    conv_b,
    skip,
    norm_gain,
    w_out,
    w_router,
    expert_ids,
    w_gate,
    w_up,
    w_down,
):
    tok_rows = tokens.shape[1]
    width = tokens.shape[2]
    heads = dt_bias.shape[0]
    inner_w = conv_w.shape[1]
    head_size = inner_w // heads
    state_size = (w_small.shape[1] - heads) // 2
    kernel = conv_w.shape[0]
    resid = tokens.reshape(tok_rows, width).astype(jnp.float32)
    normed = rms_rows(resid).astype(jnp.bfloat16)
    columns = normed
    projected = jnp.dot(
        columns, lax.all_gather(w_in, "seq", axis=0, tiled=True), preferred_element_type=jnp.float32
    )
    gate_z = projected[:, :inner_w]
    inner = projected[:, inner_w:].astype(jnp.bfloat16)
    small = jnp.dot(normed, w_small, preferred_element_type=jnp.float32)
    b_in = small[:, :state_size]
    c_out = small[:, state_size : 2 * state_size]
    step_size = jax.nn.softplus(small[:, 2 * state_size :] + dt_bias)
    rim = from_behind(inner[tok_rows - (kernel - 1) :], "seq", 1)
    padded = jnp.concatenate([rim, inner], 0).astype(jnp.float32)
    conv = conv_b + conv_w[0] * padded[0:tok_rows]
    for k in range(1, kernel):
        conv = conv + conv_w[k] * padded[k : k + tok_rows]
    signal = jax.nn.silu(conv)
    span = SCAN_BLOCK
    blocks = tok_rows // span
    log_decay = (-step_size * decay_rate).reshape(blocks, span, heads)
    step_blocks = step_size.reshape(blocks, span, heads)
    signal_blocks = signal.reshape(blocks, span, heads, head_size)
    b_blocks = b_in.reshape(blocks, span, state_size)
    c_blocks = c_out.reshape(blocks, span, state_size)
    running = jnp.cumsum(log_decay, axis=1)
    scores = jnp.einsum("zin,zjn->zij", c_blocks, b_blocks, precision=HIGHEST)
    lower = jnp.arange(span)[:, None] >= jnp.arange(span)[None, :]
    spread = running[:, :, None, :] - running[:, None, :, :]
    weight = (
        jnp.exp(jnp.where(lower[None, :, :, None], spread, -jnp.inf))
        * scores[:, :, :, None]
        * step_blocks[:, None, :, :]
    )
    within = jnp.einsum("zijh,zjhp->zihp", weight, signal_blocks, precision=HIGHEST)
    tail = jnp.exp(running[:, -1:, :] - running) * step_blocks
    block_state = jnp.einsum("zjh,zjhp,zjn->zhpn", tail, signal_blocks, b_blocks, precision=HIGHEST)
    block_decay = running[:, -1, :]
    carried = jnp.zeros((heads, head_size, state_size), jnp.float32)
    before = jnp.zeros((heads,), jnp.float32)
    starts = []
    befores = []
    for z in range(blocks):
        starts.append(carried)
        befores.append(before)
        carried = jnp.exp(block_decay[z])[:, None, None] * carried + block_state[z]
        before = before + block_decay[z]

    def link(earlier, later):
        return (earlier[0] + later[0], jnp.exp(later[0])[:, None, None] * earlier[1] + later[1])

    unused, incoming = carried_in(
        (before, carried), "seq", link, (jnp.zeros_like(before), jnp.zeros_like(carried))
    )
    entries = []
    for z in range(blocks):
        entries.append(starts[z] + jnp.exp(befores[z])[:, None, None] * incoming)
    entry = jnp.stack(entries, 0)
    across = jnp.exp(running)[..., None] * jnp.einsum(
        "zin,zhpn->zihp", c_blocks, entry, precision=HIGHEST
    )
    scanned = within + across + skip[None, None, :, None] * signal_blocks
    gated = scanned.reshape(tok_rows, inner_w) * jax.nn.silu(gate_z)
    gated = (rms_rows(gated) * norm_gain).astype(jnp.bfloat16)
    columns = gated
    mixer_sum = jnp.dot(
        columns,
        lax.all_gather(w_out, "seq", axis=0, tiled=True),
        preferred_element_type=jnp.float32,
    )
    mixed = (resid + mixer_sum).astype(jnp.bfloat16)
    routed = rms_rows(mixed.astype(jnp.float32)).astype(jnp.bfloat16)
    logits = jnp.dot(routed, w_router, preferred_element_type=jnp.float32)
    experts = w_router.shape[1]
    pair_ids = expert_ids.reshape(tok_rows * 2)
    choose = (pair_ids[:, None] == jnp.arange(experts, dtype=jnp.int32)[None, :]).astype(jnp.int32)
    picked = jnp.sum(
        choose.reshape(tok_rows, 2, experts).astype(jnp.float32) * logits[:, None, :], axis=-1
    )
    first = jax.nn.sigmoid(picked[:, 0] - picked[:, 1])
    pair_weight = jnp.stack([first, 1.0 - first], axis=1)
    earlier_hits = jnp.cumsum(choose, axis=0) - choose
    slot = jnp.sum(earlier_hits * choose, axis=1)
    members = lax.axis_size("exp")
    capacity = 6 * tok_rows // members
    target = pair_ids * capacity + slot
    outgoing = (
        jnp.zeros((experts * capacity, width), jnp.bfloat16)
        .at[target]
        .set(jnp.repeat(routed, 2, axis=0))
    )
    outgoing = outgoing.reshape(experts, capacity, width)
    arrived = lax.all_to_all(outgoing, "exp", split_axis=0, concat_axis=0, tiled=True)
    answered = expert_block(arrived.reshape(-1, width), w_gate[0], w_up[0], w_down[0])
    returned = lax.all_to_all(
        answered.reshape(members, capacity, width), "exp", split_axis=0, concat_axis=0, tiled=True
    )
    collected = returned.reshape(-1, width)[target].astype(jnp.float32).reshape(tok_rows, 2, width)
    total = mixed.astype(jnp.float32) + jnp.sum(pair_weight[:, :, None] * collected, axis=1)
    return total.astype(jnp.bfloat16).reshape(1, tok_rows, width)


def solution(mesh):
    in_specs = (
        P("exp", "seq", None),
        P("seq", None),
        P(),
        P(),
        P(),
        P(),
        P(),
        P(),
        P(),
        P("seq", None),
        P(),
        P("exp", "seq", None),
        P("exp", None, None),
        P("exp", None, None),
        P("exp", None, None),
    )
    out_specs = P("exp", "seq", None)
    return jax.shard_map(local, mesh=mesh, in_specs=in_specs, out_specs=out_specs, check_vma=False)
```

profile of v0, /device:TPU:6, one launch (start us, length us, event | category | flops | bytes accessed | tf_op | source)
XLA Modules:
  0.0 333.2 jit_solution(12080777101381084037)
XLA Ops:
  7.3 1.2 fusion.28
  8.5 1.4 fusion.43
  12.9 47.4 %all-gather.5.cloned.1.call-done = bf16[768,3072]{1,0:T(8,128)(2,1)} async-done(((bf16[48,3072]{1,0:T(8,128)(2,1)}), bf16[768,3072]{1,0:T(8,128)(2,1)}) %all-gather.5.cloned.1.call-update) | async-done | bytes 4718608 | tf_op jit(solution)/shard_map/all_gather | solution.py:73
  60.3 5.5 %fusion.60 = (bf16[256,3072]{1,0:T(8,128)(2,1)S(1)}, f32[256,3072]{1,0:T(8,128)}) fusion(bf16[768,3072]{1,0:T(8,128)(2,1)} %all-gather.5.cloned.1.call-done, bf16[1,256,768]{2,1,0:T(8,128)(2,1)S(1)} %copy-done.5, f32[256]{0:T(256)S(1)} %add_rsqrt_fusion.2), kind=kOutput, calls=%fused_computation.114 | convolution fusion | flops 1209335808 | bytes 9831424 | tf_op jit(solution)/shard_map/dot_general | solution.py:72
  65.7 2.2 collective-permute-start
  69.0 1.0 divide_multiply_fusion
  70.0 2.0 reshape.220
  72.0 2.3 copy.83
  74.4 2.5 fusion.37
  79.6 1.6 copy.84
  81.2 1.2 reduce-window.6
  82.9 19.4 %all-gather = f32[16,1,24]{2,1,0:T(1,128)} all-gather(f32[1,1,24]{2,1,0:T(1,128)} %get-tuple-element.72), channel_id=2, replica_groups=mesh['seq'=16,'exp'=32] {'seq'}, dimensions={0}, use_global_device_ids=true | all-gather | bytes 1632 | tf_op jit(solution)/shard_map/all_gather | solution.py:21
  104.1 19.8 %all-gather.7.cloned.1.call-done = f32[16,24,64,16]{2,3,1,0:T(8,128)} async-done(((f32[1,24,64,16]{2,3,1,0:T(8,128)}), f32[16,24,64,16]{2,3,1,0:T(8,128)}) %all-gather.7.cloned.1.call-update) | async-done | bytes 1572880 | tf_op jit(solution)/shard_map/all_gather | solution.py:21
  124.7 2.6 fusion.33
  127.4 7.5 %fusion.10 = f32[2,128,24,64]{1,3,2,0:T(8,128)} fusion(f32[2,128,24,64]{1,3,2,0:T(8,128)S(1)} %copy.83, f32[2,128,24,64]{1,3,2,0:T(8,128)S(1)} %fusion.33, f32[2,128,24]{1,2,0:T(8,128)S(1)} %copy-done.12, f32[2,128,128]{2,1,0:T(8,128)S(1)} %fusion.51, f32[2,128,24]{1,2,0:T(8,128)S(1)} %copy-done.10, pred[128,128]{1,0:T(8,128)(4,1)S(1)} %copy-done.14, ...), kind=kOutput, calls=%fused_computation.21 | convolution fusion | flops 608698368 | bytes 4939872 | tf_op jit(solution)/shard_map/zijh,zjhp->zihp/dot_general | solution.py:103
  134.8 3.3 copy.102
  138.1 2.8 reshape.219
  140.9 2.0 multiply_reduce_fusion.1
  142.9 24.6 %all-gather.9.cloned.1.call-done = bf16[1536,768]{1,0:T(8,128)(2,1)} async-done(((bf16[96,768]{1,0:T(8,128)(2,1)}), bf16[1536,768]{1,0:T(8,128)(2,1)}) %all-gather.9.cloned.1.call-update) | async-done | bytes 2359312 | tf_op jit(solution)/shard_map/all_gather | solution.py:136
  167.5 3.4 %multiply_reduce_fusion.2 = (f32[256]{0:T(256)S(1)}, f32[256,768]{1,0:T(8,128)S(1)}) fusion(bf16[1536,768]{1,0:T(8,128)(2,1)} %all-gather.9.cloned.1.call-done, f32[1536]{0:T(1024)S(1)} %copy-done.22, f32[256]{0:T(256)S(1)} %add_rsqrt_fusion.1, f32[256,1536]{1,0:T(8,128)S(1)} %reshape.219, f32[256,3072]{1,0:T(8,128)} %get-tuple-element.77, ...), kind=kOutput, calls=%fused_computation.49 | convolution fusion | flops 608304896 | bytes 6692864 | tf_op jit(solution)/shard_map/dot_general | solution.py:134
  173.1 1.2 reshape.213
  174.3 3.9 %scatter_custom_fusion = bf16[1536,768]{1,0:T(8,128)(2,1)S(1)} fusion(s32[512]{0:T(512)S(1)} %bitcast.120, bf16[512,768]{1,0:T(8,128)(2,1)} %reshape.213, bf16[]{:T(256)} %constant.58.clone.1), kind=kCustom, calls=%fused_computation.42 | custom fusion | bytes 2359808 | tf_op jit(solution)/shard_map/scatter | solution.py:158
  178.1 66.3 %all_to_all.10 = bf16[32,48,768]{2,1,0:T(8,128)(2,1)S(1)} all-to-all(bf16[32,48,768]{2,1,0:T(8,128)(2,1)S(1)} %bitcast.111), channel_id=1, replica_groups=mesh['seq'=16,'exp'=32] {'exp'}, dimensions={0} | all-to-all | bytes 4718592 | tf_op jit(solution)/shard_map/all_to_all | solution.py:161
  244.5 1.4 copy-done.4
  245.9 4.2 %fusion.24 = f32[1536,768]{1,0:T(8,128)} fusion(bf16[1536,768]{1,0:T(8,128)(2,1)S(1)} %bitcast.113, bf16[1,768,768]{2,1,0:T(8,128)(2,1)S(1)} %copy-done), kind=kOutput, calls=%fused_computation.40 | convolution fusion | flops 1811939328 | bytes 8257536 | tf_op jit(solution)/shard_map/dot_general | solution.py:37
  250.1 8.7 %convolution_convert_fusion = bf16[1536,768]{1,0:T(8,128)(2,1)} fusion(f32[1536,768]{1,0:T(8,128)} %fusion.24, bf16[1536,768]{1,0:T(8,128)(2,1)} %bitcast.114, bf16[1,768,768]{2,1,0:T(8,128)(2,1)S(1)} %copy-done.20, bf16[1,768,768]{2,1,0:T(8,128)(2,1)S(1)} %copy-done.21), kind=kOutput, calls=%fused_computation.5 | convolution fusion | flops 3632136192 | bytes 11796480 | tf_op jit(solution)/shard_map/dot_general | solution.py:40
  258.8 5.6 %all-to-all-start.1 = ((bf16[32,48,768]{2,1,0:T(8,128)(2,1)}), bf16[32,48,768]{2,1,0:T(8,128)(2,1)S(1)}, u32[]{:S(2)}, u32[]{:S(2)}) async-start(bf16[32,48,768]{2,1,0:T(8,128)(2,1)} %bitcast.112), calls=%async_computation.1 | async-start | bytes 4718592 | tf_op jit(solution)/shard_map/all_to_all | solution.py:163
  264.4 1.2 fusion.61
  266.5 52.5 %all-to-all-done.1 = bf16[32,48,768]{2,1,0:T(8,128)(2,1)S(1)} async-done(((bf16[32,48,768]{2,1,0:T(8,128)(2,1)}), bf16[32,48,768]{2,1,0:T(8,128)(2,1)S(1)}, u32[]{:S(2)}, u32[]{:S(2)}) %all-to-all-start.1) | async-done | bytes 2359328 | tf_op jit(solution)/shard_map/all_to_all | solution.py:163
  319.0 2.7 gather_fusion
  321.7 2.2 reshape.200
  323.9 1.9 multiply_reduce_fusion
  (101 shorter events, 14.3 us)
Async XLA Ops:
  6.5 239.4 %copy-start = (bf16[1,768,768]{2,1,0:T(8,128)(2,1)S(1)}, bf16[1,768,768]{2,1,0:T(8,128)(2,1)}, u32[]{:S(2)}) copy-start(bf16[1,768,768]{2,1,0:T(8,128)(2,1)} %param.29) | copy-start | bytes 3538948
  6.5 53.7 %copy-start.5 = (bf16[1,256,768]{2,1,0:T(8,128)(2,1)S(1)}, bf16[1,256,768]{2,1,0:T(8,128)(2,1)}, u32[]{:S(2)}) copy-start(bf16[1,256,768]{2,1,0:T(8,128)(2,1)} %param.17) | copy-start | bytes 1179652
  6.5 53.7 %all-gather.5.cloned.1.call-start = ((), (), s32[]{:S(2)}) async-start(), calls=%async_computation.2 | async-start | bytes 5013504 | tf_op jit(solution)/shard_map/all_gather | solution.py:73
  7.3 116.6 %all-gather.7.cloned.1.call-start = ((), (), s32[]{:S(2)}) async-start(), calls=%async_computation.3 | async-start | bytes 3342336 | tf_op jit(solution)/shard_map/all_gather | solution.py:21
  11.0 65.9 %copy-start.16 = (f32[24]{0:T(128)}, f32[24]{0:T(128)S(1)}, u32[]{:S(2)}) copy-start(f32[24]{0:T(128)S(1)} %broadcast_multiply_fusion.1) | copy-start | bytes 292
  12.9 55.0 %copy-start.9 = (f32[4,1536]{1,0:T(4,128)S(1)}, f32[4,1536]{1,0:T(4,128)}, u32[]{:S(2)}) copy-start(f32[4,1536]{1,0:T(4,128)} %param.22) | copy-start | bytes 73732
  65.7 3.0 collective-permute-start
  68.1 0.8 copy-start.15
  74.3 2.6 copy-start.19
  74.3 4.8 %copy-start.13 = (s32[1,256,2]{1,2,0:T(2,128)S(1)}, s32[1,256,2]{1,2,0:T(2,128)}, u32[]{:S(2)}) copy-start(s32[1,256,2]{1,2,0:T(2,128)} %param.28) | copy-start | bytes 6148
  74.4 5.2 %copy-start.8 = (f32[256,16]{0,1:T(8,128)S(1)}, f32[256,16]{0,1:T(8,128)}, u32[]{:S(2)}) copy-start(f32[256,16]{0,1:T(8,128)} %get-tuple-element.75) | copy-start | bytes 49156
  77.7 89.8 %all-gather.9.cloned.1.call-start = ((), (), s32[]{:S(2)}) async-start(), calls=%async_computation.4 | async-start | bytes 2506752 | tf_op jit(solution)/shard_map/all_gather | solution.py:136
  123.9 0.6 copy-start.17
  123.9 0.6 copy-start.18
  124.1 3.2 copy-start.10
  124.2 3.2 copy-start.11
  124.2 3.2 copy-start.12
  124.2 3.2 copy-start.14
  124.2 3.2 copy-start.23
  140.9 26.6 %copy-start.6 = (bf16[1,256,768]{2,1,0:T(8,128)(2,1)S(1)}, bf16[1,256,768]{2,1,0:T(8,128)(2,1)}, u32[]{:S(2)}) copy-start(bf16[1,256,768]{2,1,0:T(8,128)(2,1)} %param.17) | copy-start | bytes 1179652
  140.9 26.6 %copy-start.22 = (f32[1536]{0:T(1024)S(1)}, f32[1536]{0:T(1024)}, u32[]{:S(2)}) copy-start(f32[1536]{0:T(1024)} %param.25) | copy-start | bytes 18436
  170.9 0.9 copy-start.2
  171.9 0.7 copy-start.1
  244.5 1.4 copy-start.4
  245.9 4.2 %copy-start.20 = (bf16[1,768,768]{2,1,0:T(8,128)(2,1)S(1)}, bf16[1,768,768]{2,1,0:T(8,128)(2,1)}, u32[]{:S(2)}) copy-start(bf16[1,768,768]{2,1,0:T(8,128)(2,1)} %param.31) | copy-start | bytes 3538948
  245.9 4.2 %copy-start.21 = (bf16[1,768,768]{2,1,0:T(8,128)(2,1)S(1)}, bf16[1,768,768]{2,1,0:T(8,128)(2,1)}, u32[]{:S(2)}) copy-start(bf16[1,768,768]{2,1,0:T(8,128)(2,1)} %param.30) | copy-start | bytes 3538948
  258.8 60.2 %all-to-all-start.1 = ((bf16[32,48,768]{2,1,0:T(8,128)(2,1)}), bf16[32,48,768]{2,1,0:T(8,128)(2,1)S(1)}, u32[]{:S(2)}, u32[]{:S(2)}) async-start(bf16[32,48,768]{2,1,0:T(8,128)(2,1)} %bitcast.112), calls=%async_computation.1 | async-start | bytes 4718592 | tf_op jit(solution)/shard_map/all_to_all | solution.py:163
  321.7 2.2 copy-start.7
  323.9 1.9 copy-start.3
Sparse Core Ops, SparseCore 0:
  9.5 50.7 all-gather.4
  77.9 45.9 all-gather.6
  126.0 41.4 all-gather.8
where the time goes:
time: 335 us; the launch traced here: 333 us
  waiting for transfers between devices  146 us (44%)
  blocking collectives  85.7 us (26%)
  matrix products  37.3 us (11%)
  local copies, waits for them, and re-layouts  29.9 us (9%)
  between operations  13.6 us (4%)
  other arithmetic  12.4 us (4%)
  starting transfers between devices  7.82 us (2%)
    all_to_all x1, blocking collectives, local(): lax.all_to_all(outgoing, 'exp', split_axis=0, concat_axis=0, tiled=True)  66.3 us
    all_to_all x1, waiting for transfers between devices, local(): lax.all_to_all(answered.reshape(members, capacity, width), 'exp', split_a...  52.5 us
    all_gather x1, waiting for transfers between devices, local(): lax.all_gather(w_in, 'seq', axis=0, tiled=True)  47.4 us
    all_gather x1, waiting for transfers between devices, local(): lax.all_gather(w_out, 'seq', axis=0, tiled=True)  24.6 us
    all_gather x1, waiting for transfers between devices, carried_in(): gathered = jax.tree.map(lambda a: lax.all_gather(a, axis), part)  19.8 us
    all_gather x1, blocking collectives, carried_in(): gathered = jax.tree.map(lambda a: lax.all_gather(a, axis), part)  19.4 us
    dot_general x1, matrix products, expert_block(): jnp.dot(hidden.astype(jnp.bfloat16), down_mat, preferred_element_type=jnp...  8.7 us
    dot_general x1, matrix products, local(): jnp.einsum('zijh,zjhp->zihp', weight, signal_blocks, precision=HIGHEST)  7.47 us
  transfers between devices with their start and end apart: 5, of which 5 were waited for; matrix products, arithmetic and copies ran while one was open for 10% of the time, Pallas kernels for 0%

commit v1 on v0

--- a/solution.py
+++ b/solution.py
@@ -1,6 +1,8 @@
 import jax
 import jax.numpy as jnp
 from jax import lax
+from jax.experimental import pallas as pl
+from jax.experimental.pallas import tpu as pltpu
 from jax.sharding import PartitionSpec as P
 
 SCAN_BLOCK = 128
@@ -40,6 +42,264 @@
     return jnp.dot(
         hidden.astype(jnp.bfloat16), down_mat, preferred_element_type=jnp.float32
     ).astype(jnp.bfloat16)
+
+
+Y, X = 8, 4
+CAP = 48
+META = 16
+MESH = pl.DeviceIdType.MESH
+
+
+def exp_peers():
+    e = lax.axis_index("exp")
+    y, x = e // X, lax.rem(e, X)
+    return y, x
+
+
+def moe_kernel(
+    blk_ref, mixed_ref, wg_ref, wu_ref, wd_ref, out_ref,
+    gath, sbuf, arr, relay, ans, ret, back, part, rs_out, rs_in, hid,
+    ysend, yrecv, xsend, xrecv, fsend, frecv, rsend, rrecv, bsend, brecv, psend, precv,
+):
+    rows = mixed_ref.shape[0]
+    width = mixed_ref.shape[1]
+    half = rows // 2
+    slots = X * CAP
+    y, x = exp_peers()
+
+    def device(dy, dx):
+        return {"exp": lax.rem(y + dy, Y) * X + lax.rem(x + dx, X)}
+
+    up, down = device(1, 0), device(Y - 1, 0)
+
+    def remote(src, dst, send, recv, to):
+        return pltpu.make_async_remote_copy(
+            src_ref=src, dst_ref=dst, send_sem=send, recv_sem=recv,
+            device_id=to, device_id_type=MESH,
+        )
+
+    barrier = pltpu.get_barrier_semaphore()
+    for to in (up, down, device(0, 1), device(0, X - 1)):
+        pl.semaphore_signal(barrier, inc=1, device_id=to, device_id_type=MESH)
+    pl.semaphore_wait(barrier, 4)
+
+    spans = (pl.ds(0, META + half), pl.ds(META + half, half))
+
+    def right(k, h):
+        src = blk_ref if k == 1 else gath.at[k - 1]
+        return remote(src.at[spans[h]], gath.at[k, spans[h]], ysend.at[0, k - 1, h], yrecv.at[k, h], up)
+
+    def left(k, h):
+        src = blk_ref if k == 1 else gath.at[Y - k + 1]
+        return remote(src.at[spans[h]], gath.at[Y - k, spans[h]], ysend.at[1, k - 1, h], yrecv.at[Y - k, h], down)
+
+    last = Y // 2
+
+    def sent(k, h, side):
+        return k < last or (k == last and h == side)
+
+    def places(d):
+        meta = gath[d, 0:META, 0:rows].astype(jnp.float32)
+        at = []
+        for c in range(2):
+            off = meta[2 * c : 2 * c + 1, :] - (y * X).astype(jnp.float32)
+            turn = off - x.astype(jnp.float32)
+            turn = jnp.where(turn < 0.0, turn + X, turn)
+            mine = (off >= 0.0) & (off < float(X))
+            at.append(jnp.where(mine, turn * CAP + meta[2 * c + 1 : 2 * c + 2, :], -1.0))
+        line = lax.broadcasted_iota(jnp.int32, (slots, 1), 0).astype(jnp.float32)
+        return meta, line == at[0], line == at[1]
+
+    def sideways(d):
+        return 1 + (X - 2) * lax.rem(d, 2)
+
+    def dispatch(d):
+        meta, hit0, hit1 = places(d)
+        pick = jnp.where(hit0 | hit1, 1.0, 0.0).astype(jnp.bfloat16)
+        sbuf[d] = jnp.dot(pick, gath[d, META:, :], preferred_element_type=jnp.float32).astype(jnp.bfloat16)
+        arr[d, 0:CAP] = sbuf[d, 0:CAP]
+        for c in (1, 3):
+            span = pl.ds(c * CAP, CAP)
+            remote(sbuf.at[d, span], arr.at[d, span], xsend.at[d], xrecv.at[d], device(0, c)).start()
+        remote(sbuf.at[d, pl.ds(2 * CAP, CAP)], relay.at[d], xsend.at[d], frecv.at[d], device(0, sideways(d))).start()
+
+    def pass_on(d):
+        copy = remote(relay.at[d], arr.at[d, pl.ds(2 * CAP, CAP)], fsend.at[d], xrecv.at[d], device(0, sideways(d)))
+        remote(sbuf.at[d, pl.ds(2 * CAP, CAP)], relay.at[d], xsend.at[d], frecv.at[d], device(0, 1)).wait_recv()
+        copy.start()
+
+    others = pl.ds(CAP, slots - CAP)
+
+    def expert(d):
+        remote(sbuf.at[d, others], arr.at[d, others], xsend.at[d], xrecv.at[d], device(0, 1)).wait_recv()
+        tile = 256
+
+        def enter(i, carry):
+            cols = pl.ds(pl.multiple_of(i * tile, tile), tile)
+            gate = jnp.dot(arr[d], wg_ref[0, :, cols], preferred_element_type=jnp.float32)
+            lift = jnp.dot(arr[d], wu_ref[0, :, cols], preferred_element_type=jnp.float32)
+            hid[:, cols] = (gate * jax.nn.sigmoid(gate) * lift).astype(jnp.bfloat16)
+            return carry
+
+        def leave(i, carry):
+            cols = pl.ds(pl.multiple_of(i * tile, tile), tile)
+            ans[d, :, cols] = jnp.dot(hid[...], wd_ref[0, :, cols], preferred_element_type=jnp.float32).astype(jnp.bfloat16)
+            return carry
+
+        lax.fori_loop(0, wg_ref.shape[2] // tile, enter, 0)
+        lax.fori_loop(0, width // tile, leave, 0)
+        ret[d, 0:CAP] = ans[d, 0:CAP]
+        for c in (1, 3):
+            span = pl.ds(c * CAP, CAP)
+            remote(ans.at[d, span], ret.at[d, span], rsend.at[d], rrecv.at[d], device(0, X - c)).start()
+        remote(ans.at[d, pl.ds(2 * CAP, CAP)], back.at[d], rsend.at[d], brecv.at[d], device(0, sideways(d))).start()
+
+    def pass_back(d):
+        copy = remote(back.at[d], ret.at[d, pl.ds(2 * CAP, CAP)], bsend.at[d], rrecv.at[d], device(0, sideways(d)))
+        remote(ans.at[d, pl.ds(2 * CAP, CAP)], back.at[d], rsend.at[d], brecv.at[d], device(0, 1)).wait_recv()
+        copy.start()
+
+    def combine(d):
+        remote(ans.at[d, others], ret.at[d, others], rsend.at[d], rrecv.at[d], device(0, 1)).wait_recv()
+        meta, hit0, hit1 = places(d)
+        share = jnp.where(hit0, meta[4:5, :], 0.0) + jnp.where(hit1, meta[5:6, :], 0.0)
+        part[d] = lax.dot_general(
+            share.astype(jnp.bfloat16), ret[d], (((0,), (0,)), ((), ())), preferred_element_type=jnp.float32
+        )
+
+    for h in range(2):
+        right(1, h).start()
+        left(1, h).start()
+    gath[0] = blk_ref[...]
+    dispatch(0)
+
+    def both(fn, k):
+        def one(i, carry):
+            fn(k + i * (Y - 2 * k))
+            return carry
+
+        if k == 0 or k == last:
+            fn(jnp.int32(k))
+        else:
+            lax.fori_loop(0, 2, one, 0)
+
+    for k in range(1, last):
+        for h in range(2):
+            right(k, h).wait_recv()
+            if sent(k + 1, h, 0):
+                right(k + 1, h).start()
+            left(k, h).wait_recv()
+            if sent(k + 1, h, 1):
+                left(k + 1, h).start()
+        both(dispatch, k)
+        both(pass_on, k - 1)
+        both(expert, k - 1)
+        if k >= 2:
+            both(pass_back, k - 2)
+            both(combine, k - 2)
+    right(last, 0).wait_recv()
+    left(last, 1).wait_recv()
+    both(dispatch, last)
+    both(pass_on, last - 1)
+    both(expert, last - 1)
+    both(pass_on, last)
+    both(pass_back, last - 2)
+    both(expert, last)
+    both(combine, last - 2)
+    both(pass_back, last - 1)
+    both(combine, last - 1)
+    both(pass_back, last)
+    both(combine, last)
+
+    bands = (pl.ds(0, half), pl.ds(half, half))
+
+    def go(d, h, side):
+        to = down if side == 0 else up
+        land = (d - 1 if side == 0 else d + 1) if d != last else (last - 1 if side == 0 else last + 1)
+        slot = Y if land == Y else land
+        return remote(
+            rs_out.at[d, bands[h]], rs_in.at[slot, bands[h]], psend.at[d, h], precv.at[slot, h], to
+        )
+
+    rs_out[last] = part[last].astype(jnp.bfloat16)
+    go(last, 0, 0).start()
+    go(last, 1, 1).start()
+    for k in range(last - 1, 0, -1):
+        for h in range(2):
+            for side in range(2):
+                d = k if side == 0 else Y - k
+                total = part[d, bands[h]]
+                if k < last - 1 or h == side:
+                    before = (d + 1 if side == 0 else d - 1) if k < last - 1 else last
+                    go(before, h, side).wait_recv()
+                    total = total + rs_in[d, bands[h]].astype(jnp.float32)
+                rs_out[d, bands[h]] = total.astype(jnp.bfloat16)
+                go(d, h, side).start()
+    for h in range(2):
+        go(1, h, 0).wait_recv()
+        go(Y - 1, h, 1).wait_recv()
+        total = (
+            mixed_ref[bands[h]].astype(jnp.float32) + part[0, bands[h]]
+            + rs_in[0, bands[h]].astype(jnp.float32) + rs_in[Y, bands[h]].astype(jnp.float32)
+        )
+        out_ref[bands[h]] = total.astype(jnp.bfloat16)
+
+    for k in range(1, last + 1):
+        for h in range(2):
+            if sent(k, h, 0):
+                right(k, h).wait_send()
+            if sent(k, h, 1):
+                left(k, h).wait_send()
+    for d in range(Y):
+        for h in range(2):
+            if d != 0:
+                go(d, h, 0).wait_send()
+
+    def drain(d, carry):
+        remote(sbuf.at[d, others], arr.at[d, others], xsend.at[d], xrecv.at[d], device(0, 1)).wait_send()
+        remote(ans.at[d, others], ret.at[d, others], rsend.at[d], rrecv.at[d], device(0, 1)).wait_send()
+        tail = pl.ds(2 * CAP, CAP)
+        remote(relay.at[d], arr.at[d, tail], fsend.at[d], xrecv.at[d], device(0, 1)).wait_send()
+        remote(back.at[d], ret.at[d, tail], bsend.at[d], rrecv.at[d], device(0, 1)).wait_send()
+        return carry
+
+    lax.fori_loop(0, Y, drain, 0)
+
+
+def moe(blk, mixed, w_gate, w_up, w_down):
+    rows, width = mixed.shape
+    slots = X * CAP
+    bf16 = jnp.bfloat16
+    dma = pltpu.SemaphoreType.DMA
+    vmem = pl.BlockSpec(memory_space=pltpu.VMEM)
+    return pl.pallas_call(
+        moe_kernel,
+        out_shape=jax.ShapeDtypeStruct((rows, width), bf16),
+        in_specs=[vmem] * 5,
+        out_specs=vmem,
+        scratch_shapes=[
+            pltpu.VMEM((Y, META + rows, width), bf16),
+            pltpu.VMEM((Y, slots, width), bf16),
+            pltpu.VMEM((Y, slots, width), bf16),
+            pltpu.VMEM((Y, CAP, width), bf16),
+            pltpu.VMEM((Y, slots, width), bf16),
+            pltpu.VMEM((Y, slots, width), bf16),
+            pltpu.VMEM((Y, CAP, width), bf16),
+            pltpu.VMEM((Y, rows, width), jnp.float32),
+            pltpu.VMEM((Y, rows, width), bf16),
+            pltpu.VMEM((Y + 1, rows, width), bf16),
+            pltpu.VMEM((slots, w_gate.shape[2]), bf16),
+            dma((2, Y // 2, 2)), dma((Y, 2)),
+            dma((Y,)), dma((Y,)), dma((Y,)), dma((Y,)),
+            dma((Y,)), dma((Y,)), dma((Y,)), dma((Y,)),
+            dma((Y, 2)), dma((Y + 1, 2)),
+        ],
+        compiler_params=pltpu.CompilerParams(
+            collective_id=1, has_side_effects=True, vmem_limit_bytes=48 * 1024 * 1024
+        ),
+        cost_estimate=pl.CostEstimate(flops=8 * 10**9, bytes_accessed=6 * 10**6, transcendentals=10**6),
+        name="expert_exchange",
+    )(blk, mixed, w_gate, w_up, w_down)
 
 
 def local(
@@ -149,23 +409,22 @@
     pair_weight = jnp.stack([first, 1.0 - first], axis=1)
     earlier_hits = jnp.cumsum(choose, axis=0) - choose
     slot = jnp.sum(earlier_hits * choose, axis=1)
-    members = lax.axis_size("exp")
-    capacity = 6 * tok_rows // members
-    target = pair_ids * capacity + slot
-    outgoing = (
-        jnp.zeros((experts * capacity, width), jnp.bfloat16)
-        .at[target]
-        .set(jnp.repeat(routed, 2, axis=0))
-    )
-    outgoing = outgoing.reshape(experts, capacity, width)
-    arrived = lax.all_to_all(outgoing, "exp", split_axis=0, concat_axis=0, tiled=True)
-    answered = expert_block(arrived.reshape(-1, width), w_gate[0], w_up[0], w_down[0])
-    returned = lax.all_to_all(
-        answered.reshape(members, capacity, width), "exp", split_axis=0, concat_axis=0, tiled=True
-    )
-    collected = returned.reshape(-1, width)[target].astype(jnp.float32).reshape(tok_rows, 2, width)
-    total = mixed.astype(jnp.float32) + jnp.sum(pair_weight[:, :, None] * collected, axis=1)
-    return total.astype(jnp.bfloat16).reshape(1, tok_rows, width)
+    slot_of = slot.reshape(tok_rows, 2)
+    notes = jnp.stack(
+        [
+            expert_ids.reshape(tok_rows, 2)[:, 0].astype(jnp.float32),
+            slot_of[:, 0].astype(jnp.float32),
+            expert_ids.reshape(tok_rows, 2)[:, 1].astype(jnp.float32),
+            slot_of[:, 1].astype(jnp.float32),
+            first,
+            1.0 - first,
+        ],
+        axis=0,
+    )
+    notes = jnp.pad(notes, ((0, META - 6), (0, width - tok_rows))).astype(jnp.bfloat16)
+    block = jnp.concatenate([notes, routed], axis=0)
+    total = moe(block, mixed, w_gate, w_up, w_down)
+    return total.reshape(1, tok_rows, width)
 
 
 def solution(mesh):

time: 335 us -> 298 us (0.89)
  Pallas kernels: 0 us -> 113 us
  blocking collectives: 85.7 us -> 17.6 us
  waiting for transfers between devices: 146 us -> 99.4 us
  local copies, waits for them, and re-layouts: 29.9 us -> 14.7 us
  matrix products: 37.3 us -> 25.1 us
  starting transfers between devices: 7.82 us -> 2.24 us
    pallas_call x0 -> x1, Pallas kernels: none -> 113 us  [moe(): pl.pallas_call(moe_kernel, out_shape=jax.ShapeDtypeStruct((rows, width),...]
    all_to_all x1 -> x0, blocking collectives: 66.3 us -> none  [local(): lax.all_to_all(outgoing, 'exp', split_axis=0, concat_axis=0, tiled=True)]
    all_to_all x1 -> x0, waiting for transfers between devices: 52.5 us -> none  [local(): lax.all_to_all(answered.reshape(members, capacity, width), 'exp', split_a...]
    dot_general x2 -> x0, matrix products: 12.9 us -> none  [the longest x1 8.7 us: expert_block(): jnp.dot(hidden.astype(jnp.bfloat16), down_mat, preferred_element_type=jnp...]
    all_to_all x1 -> x0, starting transfers between devices: 5.58 us -> none  [local(): lax.all_to_all(answered.reshape(members, capacity, width), 'exp', split_a...]
    all_gather x1, waiting for transfers between devices: 19.8 us -> 24.4 us  [carried_in(): gathered = jax.tree.map(lambda a: lax.all_gather(a, axis), part)]
    scatter x1 -> x0, local copies, waits for them, and re-layouts: 3.87 us -> none  [local(): outgoing = jnp.zeros((experts * capacity, width), jnp.bfloat16).at[target...]
  transfers between devices with their start and end apart: 5 -> 4, of which waited for: 5 -> 3; matrix products, arithmetic and copies ran while one was open for 10% -> 9% of each run, Pallas kernels for 0% -> 0%
where the time goes in v1:
time: 298 us; the launch traced here: 296 us
  Pallas kernels  113 us (38%)
  waiting for transfers between devices  99.4 us (33%)
  matrix products  25.1 us (8%)
  blocking collectives  17.6 us (6%)
  local copies, waits for them, and re-layouts  14.7 us (5%)
  between operations  13.5 us (5%)
  other arithmetic  11 us (4%)
    pallas_call x1, Pallas kernels, moe(): pl.pallas_call(moe_kernel, out_shape=jax.ShapeDtypeStruct((rows, width),...  113 us
    all_gather x1, waiting for transfers between devices, local(): lax.all_gather(w_in, 'seq', axis=0, tiled=True)  47.4 us
    all_gather x1, waiting for transfers between devices, local(): lax.all_gather(w_out, 'seq', axis=0, tiled=True)  26.2 us
    all_gather x1, waiting for transfers between devices, carried_in(): gathered = jax.tree.map(lambda a: lax.all_gather(a, axis), part)  24.4 us
    all_gather x1, blocking collectives, carried_in(): gathered = jax.tree.map(lambda a: lax.all_gather(a, axis), part)  17.6 us
    dot_general x1, matrix products, local(): jnp.einsum('zijh,zjhp->zihp', weight, signal_blocks, precision=HIGHEST)  7.51 us
  transfers between devices with their start and end apart: 4, of which 3 were waited for; matrix products, arithmetic and copies ran while one was open for 9% of the time, Pallas kernels for 0%

profile of v1, /device:TPU:6, one launch (start us, length us, event | category | flops | bytes accessed | tf_op | source)
XLA Modules:
  0.0 296.2 jit_solution(2350661635905186063)
XLA Ops:
  6.5 0.7 all-gather.5.cloned.1.call-update
  7.3 1.2 fusion.23
  8.5 1.3 fusion.38
  9.8 0.8 negate_multiply_fusion
  11.0 0.5 broadcast_multiply_fusion
  11.5 0.6 exponential_bitcast_fusion.1
  12.2 0.6 slice_bitcast_fusion.1
  12.8 47.4 %all-gather.5.cloned.1.call-done = bf16[768,3072]{1,0:T(8,128)(2,1)} async-done(((bf16[48,3072]{1,0:T(8,128)(2,1)}), bf16[768,3072]{1,0:T(8,128)(2,1)}) %all-gather.5.cloned.1.call-update) | async-done | bytes 4718608 | tf_op jit(solution)/shard_map/all_gather | solution.py:333
  60.3 5.5 %fusion.62 = (bf16[256,3072]{1,0:T(8,128)(2,1)S(1)}, f32[256,3072]{1,0:T(8,128)}) fusion(bf16[768,3072]{1,0:T(8,128)(2,1)} %all-gather.5.cloned.1.call-done, bf16[1,256,768]{2,1,0:T(8,128)(2,1)S(1)} %copy-done.6, f32[256]{0:T(256)S(1)} %add_rsqrt_fusion.2), kind=kOutput, calls=%fused_computation.113 | convolution fusion | flops 1209335808 | bytes 9831424 | tf_op jit(solution)/shard_map/dot_general | solution.py:332
  65.7 2.2 collective-permute-start
  68.0 0.7 copy.87
  69.0 0.4 copy-done.12
  69.4 2.1 divide_multiply_fusion
  71.6 2.4 reshape.257
  74.0 2.0 copy.83
  76.0 4.0 %fusion.32 = f32[2,24,64,16]{2,3,1,0:T(8,128)S(1)} fusion(f32[2,128,24,64]{1,3,2,0:T(8,128)} %copy.83, f32[2,128,24]{1,2,0:T(8,128)} %copy.87, f32[2,128,16]{1,2,0:T(8,128)S(1)} %bitcast.104), kind=kOutput, calls=%fused_computation.48 | convolution fusion | flops 75595776 | bytes 1810432 | tf_op jit(solution)/shard_map/zjh,zjhp,zjn->zhpn/dot_general | solution.py:365
  80.1 0.8 slice_add_fusion
  80.9 0.7 all-gather.9.cloned.1.call-update
  82.2 1.2 reduce-window.6
  84.2 17.6 %all-gather = f32[16,1,24]{2,1,0:T(1,128)S(1)} all-gather(f32[1,1,24]{2,1,0:T(1,128)S(1)} %copy-done.16), channel_id=2, replica_groups=mesh['seq'=16,'exp'=32] {'seq'}, dimensions={0}, use_global_device_ids=true | all-gather | bytes 1632 | tf_op jit(solution)/shard_map/all_gather | solution.py:23
  102.3 24.4 %all-gather.7.cloned.1.call-done = f32[16,24,64,16]{2,3,1,0:T(8,128)} async-done(((f32[1,24,64,16]{2,3,1,0:T(8,128)}), f32[16,24,64,16]{2,3,1,0:T(8,128)}) %all-gather.7.cloned.1.call-update) | async-done | bytes 1572880 | tf_op jit(solution)/shard_map/all_gather | solution.py:23
  127.4 2.6 fusion.28
  130.0 7.5 %fusion.10 = f32[2,128,24,64]{1,3,2,0:T(8,128)} fusion(f32[2,128,24,64]{1,3,2,0:T(8,128)S(1)} %copy-done.5, f32[2,128,24,64]{1,3,2,0:T(8,128)S(1)} %fusion.28, f32[2,128,24]{1,2,0:T(8,128)S(1)} %copy_bitcast_fusion, f32[2,128,128]{2,1,0:T(8,128)S(1)} %fusion.50, f32[2,128,24]{1,2,0:T(8,128)S(1)} %copy.78, pred[128,128]{1,0:T(8,128)(4,1)S(1)} %iota_compare_fusion.1, ...), kind=kOutput, calls=%fused_computation.17 | convolution fusion | flops 608698368 | bytes 4939872 | tf_op jit(solution)/shard_map/zijh,zjhp->zihp/dot_general | solution.py:363
  137.5 2.2 copy.97
  139.8 1.7 reshape.256
  141.5 2.6 multiply_reduce_fusion
  144.1 26.2 %all-gather.9.cloned.1.call-done = bf16[1536,768]{1,0:T(8,128)(2,1)} async-done(((bf16[96,768]{1,0:T(8,128)(2,1)}), bf16[1536,768]{1,0:T(8,128)(2,1)}) %all-gather.9.cloned.1.call-update) | async-done | bytes 2359312 | tf_op jit(solution)/shard_map/all_gather | solution.py:396
  170.3 3.5 %fusion.21 = (f32[256]{0:T(256)S(1)}, bf16[256,768]{1,0:T(8,128)(2,1)S(1)}) fusion(bf16[1536,768]{1,0:T(8,128)(2,1)} %all-gather.9.cloned.1.call-done, f32[1536]{0:T(1024)S(1)} %copy-done.17, f32[256]{0:T(256)S(1)} %add_rsqrt_fusion.1, f32[256,1536]{1,0:T(8,128)S(1)} %copy-done.4, f32[256,3072]{1,0:T(8,128)} %get-tuple-element.81, ...), kind=kOutput, calls=%fused_computation.37 | convolution fusion | flops 608304896 | bytes 6299648 | tf_op jit(solution)/shard_map/dot_general | solution.py:394
  174.4 0.7 copy-done.1
  175.1 1.3 copy-done.3
  176.4 112.6 %expert_exchange.1 = bf16[256,768]{1,0:T(8,128)(2,1)S(1)} custom-call(bf16[272,768]{1,0:T(8,128)(2,1)S(1)} %fusion.27.blk_ref, bf16[256,768]{1,0:T(8,128)(2,1)S(1)} %get-tuple-element.83.mixed_ref, bf16[1,768,768]{2,1,0:T(8,128)(2,1)S(1)} %copy-done.1, bf16[1,768,768]{2,1,0:T(8,128)(2,1)S(1)} %copy-done.2, bf16[1,768,768]{2,1,0:T(8,128)(2,1)S(1)} %copy-done.3), custom_call_target="tpu_custom_call" | custom-call | flops 8000000000 | bytes 6000000 | tf_op jit(solution)/shard_map/expert_exchange/pallas_call | solution.py:275
  288.9 0.7 copy.124
  (81 shorter events, 3.9 us)
Async XLA Ops:
  6.5 1.9 copy-start
  6.5 53.7 %copy-start.6 = (bf16[1,256,768]{2,1,0:T(8,128)(2,1)S(1)}, bf16[1,256,768]{2,1,0:T(8,128)(2,1)}, u32[]{:S(2)}) copy-start(bf16[1,256,768]{2,1,0:T(8,128)(2,1)} %param.17) | copy-start | bytes 1179652
  6.5 53.7 %all-gather.5.cloned.1.call-start = ((), (), s32[]{:S(2)}) async-start(), calls=%async_computation | async-start | bytes 5013504 | tf_op jit(solution)/shard_map/all_gather | solution.py:333
  7.3 119.4 %all-gather.7.cloned.1.call-start = ((), (), s32[]{:S(2)}) async-start(), calls=%async_computation.1 | async-start | bytes 3342336 | tf_op jit(solution)/shard_map/all_gather | solution.py:23
  12.8 55.1 %copy-start.10 = (f32[4,1536]{1,0:T(4,128)S(1)}, f32[4,1536]{1,0:T(4,128)}, u32[]{:S(2)}) copy-start(f32[4,1536]{1,0:T(4,128)} %param.22) | copy-start | bytes 73732
  65.7 3.0 %collective-permute-start = (bf16[3,1536]{1,0:T(4,128)(2,1)S(1)}, bf16[3,1536]{1,0:T(4,128)(2,1)S(1)}, u32[]{:S(2)}, u32[]{:S(2)}) collective-permute-start(bf16[3,1536]{1,0:T(4,128)(2,1)S(1)} %slice.122), channel_id=1, source_target_pairs={{0,32},{32,64},{64,96},{96,128},{128,160},{160,192},{192,224},{224... | collective-permute-start | bytes 27656 | tf_op jit(solution)/shard_map/ppermute | solution.py:18
  68.7 0.7 copy-start.12
  76.0 4.0 %copy-start.13 = (f32[24]{0:T(128)S(1)}, f32[24]{0:T(128)}, u32[]{:S(2)}) copy-start(f32[24]{0:T(128)} %broadcast_multiply_fusion) | copy-start | bytes 292
  76.0 4.0 %copy-start.15 = (f32[24]{0:T(128)S(1)}, f32[24]{0:T(128)}, u32[]{:S(2)}) copy-start(f32[24]{0:T(128)} %get-tuple-element.73) | copy-start | bytes 292
  76.0 5.6 %copy-start.11 = (s32[1,256,2]{1,2,0:T(2,128)S(1)}, s32[1,256,2]{1,2,0:T(2,128)}, u32[]{:S(2)}) copy-start(s32[1,256,2]{1,2,0:T(2,128)} %param.28) | copy-start | bytes 6148
  76.0 6.1 %copy-start.8 = (f32[256,16]{0,1:T(8,128)S(1)}, f32[256,16]{0,1:T(8,128)}, u32[]{:S(2)}) copy-start(f32[256,16]{0,1:T(8,128)} %get-tuple-element.77) | copy-start | bytes 49156
  80.0 4.2 %copy-start.16 = (f32[1,1,24]{2,1,0:T(1,128)S(1)}, f32[1,1,24]{2,1,0:T(1,128)}, u32[]{:S(2)}) copy-start(f32[1,1,24]{2,1,0:T(1,128)} %get-tuple-element.74) | copy-start | bytes 292
  80.0 21.8 %copy-start.7 = (f32[2,2,8,128]{3,2,1,0:T(8,128)S(1)}, f32[2,2,8,128]{3,2,1,0:T(8,128)}, u32[]{:S(2)}) copy-start(f32[2,2,8,128]{3,2,1,0:T(8,128)} %get-tuple-element.75) | copy-start | bytes 49156
  80.9 89.4 %all-gather.9.cloned.1.call-start = ((), (), s32[]{:S(2)}) async-start(), calls=%async_computation.2 | async-start | bytes 2506752 | tf_op jit(solution)/shard_map/all_gather | solution.py:396
  126.6 0.6 copy-start.14
  126.8 3.2 %copy-start.5 = (f32[2,128,24,64]{1,3,2,0:T(8,128)S(1)}, f32[2,128,24,64]{1,3,2,0:T(8,128)}, u32[]{:S(2)}) copy-start(f32[2,128,24,64]{1,3,2,0:T(8,128)} %copy.83) | copy-start | bytes 4718596
  126.9 3.2 %copy-start.18 = (f32[24]{0:T(128)S(1)}, f32[24]{0:T(128)}, u32[]{:S(2)}) copy-start(f32[24]{0:T(128)} %param.24) | copy-start | bytes 292
  141.5 28.8 %copy-start.4 = (f32[256,1536]{1,0:T(8,128)S(1)}, f32[256,1536]{1,0:T(8,128)}, u32[]{:S(2)}) copy-start(f32[256,1536]{1,0:T(8,128)} %reshape.256) | copy-start | bytes 4718596
  141.5 28.8 %copy-start.17 = (f32[1536]{0:T(1024)S(1)}, f32[1536]{0:T(1024)}, u32[]{:S(2)}) copy-start(f32[1536]{0:T(1024)} %param.25) | copy-start | bytes 18436
  144.1 29.9 %copy-start.9 = (bf16[768,32]{0,1:T(8,128)(2,1)S(1)}, bf16[768,32]{0,1:T(8,128)(2,1)}, u32[]{:S(2)}) copy-start(bf16[768,32]{0,1:T(8,128)(2,1)} %param.27) | copy-start | bytes 147460
  170.3 4.1 %copy-start.2 = (bf16[1,768,768]{2,1,0:T(8,128)(2,1)S(1)}, bf16[1,768,768]{2,1,0:T(8,128)(2,1)}, u32[]{:S(2)}) copy-start(bf16[1,768,768]{2,1,0:T(8,128)(2,1)} %wu_ref.1) | copy-start | bytes 3538948
  173.8 1.3 copy-start.1
  175.1 1.3 copy-start.3
Sparse Core Ops, SparseCore 0:
  9.5 50.7 all-gather.4
  81.0 45.5 all-gather.6
  128.8 41.4 all-gather.8

commit v2 on v1

--- a/solution.py
+++ b/solution.py
@@ -4,45 +4,6 @@
 from jax.experimental import pallas as pl
 from jax.experimental.pallas import tpu as pltpu
 from jax.sharding import PartitionSpec as P
-
-SCAN_BLOCK = 128
-
-
-EPSILON = 1e-05
-HIGHEST = lax.Precision.HIGHEST
-
-
-def from_behind(block, axis, distance):
-    devices = range(lax.axis_size(axis))
-    route = [(i - distance, i) for i in devices if i - distance in devices]
-    return lax.ppermute(block, axis, route)
-
-
-def carried_in(part, axis, combine, identity):
-    place = lax.axis_index(axis)
-    gathered = jax.tree.map(lambda a: lax.all_gather(a, axis), part)
-    state = jax.tree.map(lambda a, e: jnp.zeros_like(a) + jnp.asarray(e, a.dtype), part, identity)
-
-    def one(lap, state):
-        return combine(
-            state, jax.tree.map(lambda a: lax.dynamic_index_in_dim(a, lap, 0, False), gathered)
-        )
-
-    return lax.fori_loop(0, place, one, state)
-
-
-def rms_rows(values):
-    return values * lax.rsqrt(jnp.mean(values * values, axis=-1, keepdims=True) + EPSILON)
-
-
-def expert_block(rows_in, gate_mat, up_mat, down_mat):
-    hidden = jax.nn.silu(jnp.dot(rows_in, gate_mat, preferred_element_type=jnp.float32)) * jnp.dot(
-        rows_in, up_mat, preferred_element_type=jnp.float32
-    )
-    return jnp.dot(
-        hidden.astype(jnp.bfloat16), down_mat, preferred_element_type=jnp.float32
-    ).astype(jnp.bfloat16)
-
 
 Y, X = 8, 4
 CAP = 48
@@ -302,6 +263,546 @@
     )(blk, mixed, w_gate, w_up, w_down)
 
 
+Z = 8
+HALO = 16
+EPSILON = 1e-05
+HIGHEST = lax.Precision.HIGHEST
+F32 = jnp.float32
+BF16 = jnp.bfloat16
+
+
+def mixer_kernel(
+    tok_ref, win_ref, wsmall_ref, dtb_ref, rate_ref, cw_ref, cb_ref, skip_ref, gain_ref, wout_ref, wr_ref, ids_ref,
+    mixed_ref, blk_ref,
+    wi, wo, normed, ext, sig, gz, step_l, tail_l, run_l, wmat, bmat, cmat, yy, decs, dec_out, states, state_out,
+    gg, half_out, half_in, notes,
+    isend, irecv, nsend, nrecv, osend, orecv, mosend, morecv, dsend, drecv, ssend, srecv, misc_send, misc_recv,
+):
+    rows, width = tok_ref.shape
+    both = 2 * rows
+    inner_w = wi.shape[1] // 2
+    heads = skip_ref.shape[1] // 2
+    head_size = inner_w // heads
+    n_state = (wsmall_ref.shape[1] - 2 * heads) // 2
+    in_rows = win_ref.shape[0]
+    out_rows = wout_ref.shape[0]
+    part = inner_w // 2
+    seat = lax.axis_index("seq")
+    z, c = seat // 2, lax.rem(seat, 2)
+    y, x = exp_peers()
+    pair = lax.rem(y, 2), lax.rem(x, 2)
+
+    def device(dz=0, core=None, dy=0, dx=0):
+        return {
+            "seq": lax.rem(z + dz, Z) * 2 + (c if core is None else core),
+            "exp": lax.rem(y + dy, Y) * X + lax.rem(x + dx, X),
+        }
+
+    sibling = device(core=1 - c)
+
+    def remote(src, dst, send, recv, to):
+        return pltpu.make_async_remote_copy(
+            src_ref=src, dst_ref=dst, send_sem=send, recv_sem=recv, device_id=to, device_id_type=MESH
+        )
+
+    barrier = pltpu.get_barrier_semaphore()
+    peers = [sibling, device(dy=1), device(dy=Y - 1), device(dx=1), device(dx=X - 1)]
+    peers += [device(dz=j) for j in range(1, Z)]
+    for to in peers:
+        pl.semaphore_signal(barrier, inc=1, device_id=to, device_id_type=MESH)
+    pl.semaphore_wait(barrier, len(peers))
+
+    def lanes(start, size):
+        return pl.ds(pl.multiple_of(start, 128), size)
+
+    def in_band(zs, h):
+        return pl.ds(pl.multiple_of((2 * zs + h) * in_rows, 16), in_rows)
+
+    def out_band(zs, h):
+        return pl.ds(pl.multiple_of(lax.rem(2 * zs + h, Z) * out_rows, 16), out_rows)
+
+    first_in = lanes(pair[0] * part, part)
+    second_in = lanes(inner_w + pair[1] * part, part)
+    first_out = lanes(pair[1] * part, part)
+
+    def origin(k, side):
+        return lax.rem(z + Z - k, Z) if side == 0 else lax.rem(z + k, Z)
+
+    def landed(k, side):
+        return k if side == 0 else Z - k
+
+    def hop(k, h, side):
+        band = in_band(origin(k - 1, side), h)
+        to = device(dz=1 if side == 0 else Z - 1)
+        return [
+            remote(wi.at[band, cols], wi.at[band, cols], isend.at[side, k - 1, h], irecv.at[landed(k, side), h], to)
+            for cols in (first_in, second_in)
+        ]
+
+    def in_whole(send, recv):
+        return remote(wi.at[0:in_rows, 0:inner_w], wi.at[0:in_rows, 0:inner_w], send, recv, sibling)
+
+    def hop_arrived(k, h, side):
+        in_whole(isend.at[side, k - 1, h], irecv.at[landed(k, side), h]).wait_recv()
+
+    def share(k, h, side):
+        band = in_band(origin(k, side), h)
+        off = landed(k, side)
+        for cols, to in (
+            (first_in, device(dy=1 if h == 0 else Y - 1)),
+            (second_in, device(dx=1 if h == 0 else X - 1)),
+        ):
+            remote(wi.at[band, cols], wi.at[band, cols], nsend.at[off, h], nrecv.at[off, h], to).start()
+
+    def out_hop(k, h, side):
+        band = out_band(origin(k - 1, side), h)
+        to = device(dz=1 if side == 0 else Z - 1)
+        return remote(
+            wo.at[band, first_out], wo.at[band, first_out], osend.at[side, k - 1, h], orecv.at[landed(k, side), h], to
+        )
+
+    def out_share(k, h, side):
+        band = out_band(origin(k, side), h)
+        off = landed(k, side)
+        return remote(
+            wo.at[band, first_out], wo.at[band, first_out], mosend.at[off, h], morecv.at[off, h],
+            device(dx=1 if h == 0 else X - 1),
+        )
+
+    last = Z // 2
+
+    def sent(k, h, side):
+        return k < last or (k == last and h == side)
+
+    def wanted(k, side):
+        return origin(k, side) // last == c
+
+    def units(k):
+        return [(h, side) for h in range(2) for side in range(2) if sent(k, h, side)]
+
+    wi[in_band(z, c), 0:inner_w] = win_ref[:, lanes(2 * inner_w + c * inner_w, inner_w)]
+    wi[in_band(z, c), inner_w:] = win_ref[:, lanes(c * inner_w, inner_w)]
+
+    def to_sibling():
+        return [
+            remote(
+                win_ref.at[:, lanes(base + (1 - c) * inner_w, inner_w)],
+                wi.at[in_band(z, c), pl.ds(at, inner_w)],
+                misc_send.at[0], misc_recv.at[0], sibling,
+            )
+            for base, at in ((2 * inner_w, 0), (0, inner_w))
+        ]
+
+    for copy in to_sibling():
+        copy.start()
+    for side in range(2):
+        for copy in hop(1, c, side):
+            copy.start()
+
+    def out_to_sibling():
+        return remote(wout_ref, wo.at[out_band(z, c)], misc_send.at[4], misc_recv.at[4], sibling)
+
+    home = z // last == c
+
+    @pl.when(home)
+    def _():
+        wo[out_band(z, c), :] = wout_ref[...]
+
+    @pl.when(jnp.logical_not(home))
+    def _():
+        out_to_sibling().start()
+
+    resid = tok_ref[...].astype(F32)
+    scale = lax.rsqrt(jnp.mean(resid * resid, axis=-1, keepdims=True) + EPSILON)
+    mine = pl.ds(pl.multiple_of(HALO + c * rows, 16), rows)
+    normed[mine, :] = (resid * scale).astype(BF16)
+
+    def rows_across():
+        return remote(normed.at[mine], normed.at[mine], misc_send.at[1], misc_recv.at[1], sibling)
+
+    rows_across().start()
+    other_in = remote(
+        wi.at[0:in_rows], wi.at[0:in_rows], misc_send.at[0], misc_recv.at[0], sibling
+    )
+    other_in.wait_recv()
+    for side in range(2):
+        for copy in hop(1, 1 - c, side):
+            copy.start()
+
+    rows_across().wait_recv()
+
+    def halo():
+        return remote(
+            normed.at[both : both + HALO], normed.at[0:HALO], misc_send.at[2], misc_recv.at[2], device(dz=1)
+        )
+
+    @pl.when(z < Z - 1)
+    def _():
+        halo().start()
+
+    @pl.when(z == 0)
+    def _():
+        normed[0:HALO, :] = jnp.zeros((HALO, width), BF16)
+
+    small = jnp.dot(normed[HALO:, :], wsmall_ref[...], preferred_element_type=F32)
+    bmat[...] = small[:, 0:n_state]
+    cmat[...] = small[:, n_state : 2 * n_state]
+    raw = small[:, 2 * n_state :] + dtb_ref[...]
+    step_all = jnp.maximum(raw, 0.0) + jnp.log1p(jnp.exp(-jnp.abs(raw)))
+    decay_all = -step_all * rate_ref[...]
+
+    def own_heads(v):
+        return jnp.where(c == 0, v[:, 0:heads], v[:, heads : 2 * heads])
+
+    step = own_heads(step_all)
+    log_decay = own_heads(decay_all)
+    head_of = lax.broadcasted_iota(jnp.int32, (heads, inner_w), 1) // head_size
+    spread = (head_of == lax.broadcasted_iota(jnp.int32, (heads, inner_w), 0)).astype(BF16)
+    spread_f = spread.astype(F32)
+
+    def expand(v):
+        high = v.astype(BF16)
+        low = (v - high.astype(F32)).astype(BF16)
+        return jnp.dot(high, spread, preferred_element_type=F32) + jnp.dot(low, spread, preferred_element_type=F32)
+
+    row_id = lax.broadcasted_iota(jnp.int32, (rows, rows), 0)
+    col_id = lax.broadcasted_iota(jnp.int32, (rows, rows), 1)
+    lower = (row_id >= col_id).astype(F32)
+    upper = (row_id <= col_id).astype(F32)
+    running, running_t, ends, scores = [], [], [], []
+    for q in range(2):
+        piece = log_decay[q * rows : (q + 1) * rows]
+        run = jnp.dot(lower, piece, precision=HIGHEST, preferred_element_type=F32)
+        running.append(run)
+        running_t.append(
+            lax.dot_general(piece, upper, (((0,), (0,)), ((), ())), precision=HIGHEST, preferred_element_type=F32)
+        )
+        end = run[rows - 1 : rows]
+        ends.append(end)
+        span = pl.ds(q * rows, rows)
+        here = step[q * rows : (q + 1) * rows]
+        step_l[span, :] = expand(here)
+        tail_l[span, :] = expand(here * jnp.exp(end - run))
+        run_l[span, :] = expand(jnp.exp(run))
+        grid = lax.dot_general(
+            cmat[span, :], bmat[span, :], (((1,), (1,)), ((), ())), precision=HIGHEST, preferred_element_type=F32
+        )
+        scores.append(jnp.where(row_id >= col_id, grid, 0.0))
+    ends_l = [
+        jnp.dot(jnp.broadcast_to(end, (8, heads)), spread_f, precision=HIGHEST, preferred_element_type=F32)
+        for end in ends
+    ]
+    dec_out[...] = ends_l[0] + ends_l[1]
+
+    def decay_copy(j):
+        return remote(dec_out, decs.at[j], dsend.at[j], drecv.at[j], device(dz=j))
+
+    def state_copy(j):
+        return remote(state_out, states.at[j], ssend.at[j], srecv.at[j], device(dz=j))
+
+    for j in range(1, Z):
+
+        @pl.when(z + j < Z)
+        def _(j=j):
+            decay_copy(j).start()
+
+    def advance(k):
+        for h, side in units(k):
+            hop_arrived(k, h, side)
+            if k < last and sent(k + 1, h, side):
+                for copy in hop(k + 1, h, side):
+                    copy.start()
+            share(k, h, side)
+
+    def weigh(q):
+        for i in range(heads):
+            gap = jnp.minimum(running[q][:, i : i + 1] - running_t[q][i : i + 1, :], 0.0)
+            wmat[q * heads + i] = (jnp.exp(gap) * scores[q]).astype(BF16)
+
+    advance(1)
+    weigh(0)
+    advance(2)
+    weigh(1)
+    advance(3)
+
+    experts = wr_ref.shape[1]
+    lane = lax.broadcasted_iota(jnp.int32, (rows, experts), 1)
+    hits = [lane == ids_ref[:, k : k + 1] for k in range(2)]
+    taken = (hits[0] | hits[1]).astype(F32).astype(BF16)
+    before = jnp.dot((row_id > col_id).astype(F32).astype(BF16), taken, preferred_element_type=F32)
+    place = [jnp.sum(jnp.where(hit, before, 0.0), axis=1, keepdims=True) for hit in hits]
+    number = [jnp.sum(jnp.where(hit, lane.astype(F32), 0.0), axis=1, keepdims=True) for hit in hits]
+    wide = lax.broadcasted_iota(jnp.int32, (rows, 128), 1)
+    table = jnp.where(wide == 0, number[0], 0.0)
+    table = jnp.where(wide == 1, place[0], table)
+    table = jnp.where(wide == 2, number[1], table)
+    notes[...] = jnp.where(wide == 3, place[1], table)
+
+    advance(last)
+    for k in range(1, last + 1):
+        for h, side in units(k):
+            off = landed(k, side)
+            in_whole(nsend.at[off, h], nrecv.at[off, h]).wait_recv()
+
+    @pl.when(home)
+    def _():
+        out_to_sibling().wait_recv()
+        for h, side in units(1):
+            out_hop(1, h, side).start()
+
+    def out_advance(k):
+        for h, side in units(k):
+
+            @pl.when(wanted(k, side))
+            def _(h=h, side=side):
+                out_hop(k, h, side).wait_recv()
+                if k < last and sent(k + 1, h, side):
+                    out_hop(k + 1, h, side).start()
+                out_share(k, h, side).start()
+
+    @pl.when(z > 0)
+    def _():
+        halo().wait_recv()
+
+    tile = 256
+
+    def project(i, carry):
+        cols = pl.ds(pl.multiple_of(i * tile, tile), tile)
+        ext[:, cols] = jnp.dot(normed[...], wi[:, cols], preferred_element_type=F32).astype(BF16).astype(F32)
+        return carry
+
+    lax.fori_loop(0, inner_w // tile, project, 0)
+    taps = cw_ref.shape[0]
+
+    def convolve(i, carry):
+        cols = pl.ds(pl.multiple_of(i * 128, 128), 128)
+        params = lanes(c * inner_w + i * 128, 128)
+        for q in range(2):
+            acc = cb_ref[:, params] + jnp.zeros((rows, 128), F32)
+            for k in range(taps):
+                acc = acc + cw_ref[k : k + 1, params] * ext[pl.ds(HALO - taps + 1 + k + q * rows, rows), cols]
+            sig[pl.ds(q * rows, rows), cols] = acc * jax.nn.sigmoid(acc)
+        return carry
+
+    lax.fori_loop(0, inner_w // 128, convolve, 0)
+    own_state = []
+    for q in range(2):
+        span = pl.ds(q * rows, rows)
+        own_state.append(
+            lax.dot_general(
+                bmat[span, :].astype(BF16), (sig[span, :] * tail_l[span, :]).astype(BF16), (((0,), (0,)), ((), ())),
+                preferred_element_type=F32,
+            )
+        )
+    state_out[...] = (jnp.exp(ends_l[1][0:1]) * own_state[0] + own_state[1]).astype(BF16)
+    for j in range(1, Z):
+
+        @pl.when(z + j < Z)
+        def _(j=j):
+            state_copy(j).start()
+
+        @pl.when(z < j)
+        def _(j=j):
+            states[j] = jnp.zeros_like(state_out)
+            decs[j] = jnp.zeros_like(dec_out)
+
+    out_advance(1)
+
+    def project_gate(i, carry):
+        cols = pl.ds(pl.multiple_of(i * tile, tile), tile)
+        weight = wi[:, pl.ds(pl.multiple_of(inner_w + i * tile, tile), tile)]
+        gz[:, cols] = jnp.dot(normed[HALO:, :], weight, preferred_element_type=F32)
+        return carry
+
+    lax.fori_loop(0, inner_w // tile, project_gate, 0)
+    out_advance(2)
+    left_lane = lax.broadcasted_iota(jnp.int32, (rows, 128), 1) < head_size
+
+    def within(p, carry):
+        cols = pl.ds(pl.multiple_of(p * 128, 128), 128)
+        skips = jnp.sum(
+            jnp.where(
+                lax.broadcasted_iota(jnp.int32, (heads * 2, 128), 0)
+                == c * heads + 2 * p + lax.broadcasted_iota(jnp.int32, (heads * 2, 128), 1) // head_size,
+                jnp.broadcast_to(skip_ref[...], (128, heads * 2)).T, 0.0,
+            ),
+            axis=0, keepdims=True,
+        )
+        for q in range(2):
+            span = pl.ds(q * rows, rows)
+            fresh = (sig[span, cols] * step_l[span, cols]).astype(BF16)
+            a = jnp.dot(wmat[q * heads + 2 * p], fresh, preferred_element_type=F32)
+            b = jnp.dot(wmat[q * heads + 2 * p + 1], fresh, preferred_element_type=F32)
+            yy[span, cols] = jnp.where(left_lane, a, b) + skips * sig[span, cols]
+        return carry
+
+    lax.fori_loop(0, inner_w // 128, within, 0)
+    out_advance(3)
+    out_advance(last)
+
+    entry = jnp.zeros((n_state, inner_w), F32)
+    lead = jnp.zeros((1, inner_w), F32)
+    for j in range(1, Z):
+
+        @pl.when(z >= j)
+        def _(j=j):
+            decay_copy(j).wait_recv()
+            state_copy(j).wait_recv()
+
+        entry = entry + jnp.exp(lead) * states[j].astype(F32)
+        lead = lead + decs[j, 0:1]
+    gain = gain_ref[:, lanes(c * inner_w, inner_w)]
+    squares = []
+    for q in range(2):
+        span = pl.ds(q * rows, rows)
+        start = entry if q == 0 else jnp.exp(ends_l[0][0:1]) * entry + own_state[0]
+        across = run_l[span, :] * jnp.dot(cmat[span, :].astype(BF16), start.astype(BF16), preferred_element_type=F32)
+        gate = gz[span, :]
+        gated = (yy[span, :] + across) * (gate * jax.nn.sigmoid(gate))
+        squares.append(jnp.sum(gated * gated, axis=1, keepdims=True))
+        gg[span, :] = (gated * gain).astype(BF16)
+
+    @pl.when(home)
+    def _():
+        pass
+
+    for k in range(1, last + 1):
+        for h, side in units(k):
+
+            @pl.when(wanted(k, side))
+            def _(k=k, h=h, side=side):
+                out_share(k, h, side).wait_recv()
+
+    theirs = pl.ds(pl.multiple_of((1 - c) * rows, 16), rows)
+    ours = pl.ds(pl.multiple_of(c * rows, 16), rows)
+
+    def leave(i, carry):
+        cols = pl.ds(pl.multiple_of(i * tile, tile), tile)
+        half_out[:, cols] = jnp.dot(gg[theirs, :], wo[:, cols], preferred_element_type=F32).astype(BF16)
+        return carry
+
+    lax.fori_loop(0, width // tile, leave, 0)
+    their_square = jnp.where(c == 0, squares[1], squares[0])
+    our_square = jnp.where(c == 0, squares[0], squares[1])
+    high = their_square.astype(BF16).astype(F32)
+    half_out[:, width:] = jnp.where(wide < 64, high, their_square - high).astype(BF16)
+
+    def halves():
+        return remote(half_out, half_in, misc_send.at[3], misc_recv.at[3], sibling)
+
+    halves().start()
+
+    def stay(i, carry):
+        cols = pl.ds(pl.multiple_of(i * tile, tile), tile)
+        yy[0:rows, cols] = jnp.dot(gg[ours, :], wo[:, cols], preferred_element_type=F32)
+        return carry
+
+    lax.fori_loop(0, width // tile, stay, 0)
+    halves().wait_recv()
+    extra = half_in[:, width:].astype(F32)
+    total = our_square + extra[:, 0:1] + extra[:, 64:65]
+    norm = lax.rsqrt(total / (2 * inner_w) + EPSILON)
+    mixed = (
+        tok_ref[...].astype(F32) + norm * (yy[0:rows, 0:width] + half_in[:, 0:width].astype(F32))
+    ).astype(BF16)
+    mixed_ref[...] = mixed
+    mixed_f = mixed.astype(F32)
+    routed = (mixed_f * lax.rsqrt(jnp.mean(mixed_f * mixed_f, axis=-1, keepdims=True) + EPSILON)).astype(BF16)
+    blk_ref[META:, :] = routed
+    logits = jnp.dot(routed, wr_ref[...], preferred_element_type=F32)
+    picked = [
+        jnp.sum(jnp.where(lane == ids_ref[:, k : k + 1], logits, 0.0), axis=1, keepdims=True) for k in range(2)
+    ]
+    first = jax.nn.sigmoid(picked[0] - picked[1])
+    table = jnp.where(wide == 4, first, notes[...])
+    table = jnp.where(wide == 5, 1.0 - first, table)
+    blk_ref[0:META, 0:rows] = table.T[0:META, :].astype(BF16)
+    blk_ref[0:META, rows:] = jnp.zeros((META, width - rows), BF16)
+
+    for copy in (other_in, rows_across(), halves()):
+        copy.wait_send()
+
+    @pl.when(z < Z - 1)
+    def _():
+        halo().wait_send()
+
+    @pl.when(jnp.logical_not(home))
+    def _():
+        out_to_sibling().wait_send()
+
+    for k in range(1, last + 1):
+        for h, side in units(k):
+            off = landed(k, side)
+            in_whole(isend.at[side, k - 1, h], irecv.at[off, h]).wait_send()
+            in_whole(nsend.at[off, h], nrecv.at[off, h]).wait_send()
+
+            @pl.when(wanted(k - 1, side))
+            def _(k=k, h=h, side=side):
+                out_hop(k, h, side).wait_send()
+
+            @pl.when(wanted(k, side))
+            def _(k=k, h=h, side=side):
+                out_share(k, h, side).wait_send()
+
+    for j in range(1, Z):
+
+        @pl.when(z + j < Z)
+        def _(j=j):
+            decay_copy(j).wait_send()
+            state_copy(j).wait_send()
+
+
+def mixer(tokens, w_in, w_small, dt_bias, decay_rate, conv_w, conv_b, skip, norm_gain, w_out, w_router, ids):
+    rows, width = tokens.shape
+    inner_w = conv_w.shape[1] // 2
+    heads = dt_bias.shape[0] // 2
+    n_state = (w_small.shape[1] - 2 * heads) // 2
+    both = 2 * rows
+    dma = pltpu.SemaphoreType.DMA
+    vmem = pl.BlockSpec(memory_space=pltpu.VMEM)
+    wide = pltpu.VMEM((both, inner_w), F32)
+    line = lambda v: v.reshape(1, -1)
+    return pl.pallas_call(
+        mixer_kernel,
+        out_shape=(
+            jax.ShapeDtypeStruct((rows, width), BF16),
+            jax.ShapeDtypeStruct((META + rows, width), BF16),
+        ),
+        in_specs=[vmem] * 12,
+        out_specs=(vmem, vmem),
+        scratch_shapes=[
+            pltpu.VMEM((width, 2 * inner_w), BF16),
+            pltpu.VMEM((inner_w, width), BF16),
+            pltpu.VMEM((HALO + both, width), BF16),
+            pltpu.VMEM((HALO + both, inner_w), F32),
+            wide, wide, wide, wide, wide,
+            pltpu.VMEM((2 * heads, rows, rows), BF16),
+            pltpu.VMEM((both, n_state), F32),
+            pltpu.VMEM((both, n_state), F32),
+            wide,
+            pltpu.VMEM((Z, 8, inner_w), F32),
+            pltpu.VMEM((8, inner_w), F32),
+            pltpu.VMEM((Z, n_state, inner_w), BF16),
+            pltpu.VMEM((n_state, inner_w), BF16),
+            pltpu.VMEM((both, inner_w), BF16),
+            pltpu.VMEM((rows, width + 128), BF16),
+            pltpu.VMEM((rows, width + 128), BF16),
+            pltpu.VMEM((rows, 128), F32),
+            dma((2, Z // 2, 2)), dma((Z, 2)), dma((Z, 2)), dma((Z, 2)),
+            dma((2, Z // 2, 2)), dma((Z, 2)), dma((Z, 2)), dma((Z, 2)),
+            dma((Z,)), dma((Z,)), dma((Z,)), dma((Z,)),
+            dma((5,)), dma((5,)),
+        ],
+        compiler_params=pltpu.CompilerParams(
+            collective_id=2, has_side_effects=True, vmem_limit_bytes=48 * 1024 * 1024
+        ),
+        name="state_space_mixer",
+    )(
+        tokens, w_in, w_small, line(dt_bias), line(decay_rate), conv_w, line(conv_b), line(skip), line(norm_gain),
+        w_out, w_router, ids,
+    )
+
+
 def local(
     tokens,
     w_in,
@@ -319,112 +820,10 @@
     w_up,
     w_down,
 ):
-    tok_rows = tokens.shape[1]
-    width = tokens.shape[2]
-    heads = dt_bias.shape[0]
-    inner_w = conv_w.shape[1]
-    head_size = inner_w // heads
-    state_size = (w_small.shape[1] - heads) // 2
-    kernel = conv_w.shape[0]
-    resid = tokens.reshape(tok_rows, width).astype(jnp.float32)
-    normed = rms_rows(resid).astype(jnp.bfloat16)
-    columns = normed
-    projected = jnp.dot(
-        columns, lax.all_gather(w_in, "seq", axis=0, tiled=True), preferred_element_type=jnp.float32
+    mixed, block = mixer(
+        tokens[0], w_in, w_small, dt_bias, decay_rate, conv_w, conv_b, skip, norm_gain, w_out, w_router, expert_ids[0]
     )
-    gate_z = projected[:, :inner_w]
-    inner = projected[:, inner_w:].astype(jnp.bfloat16)
-    small = jnp.dot(normed, w_small, preferred_element_type=jnp.float32)
-    b_in = small[:, :state_size]
-    c_out = small[:, state_size : 2 * state_size]
-    step_size = jax.nn.softplus(small[:, 2 * state_size :] + dt_bias)
-    rim = from_behind(inner[tok_rows - (kernel - 1) :], "seq", 1)
-    padded = jnp.concatenate([rim, inner], 0).astype(jnp.float32)
-    conv = conv_b + conv_w[0] * padded[0:tok_rows]
-    for k in range(1, kernel):
-        conv = conv + conv_w[k] * padded[k : k + tok_rows]
-    signal = jax.nn.silu(conv)
-    span = SCAN_BLOCK
-    blocks = tok_rows // span
-    log_decay = (-step_size * decay_rate).reshape(blocks, span, heads)
-    step_blocks = step_size.reshape(blocks, span, heads)
-    signal_blocks = signal.reshape(blocks, span, heads, head_size)
-    b_blocks = b_in.reshape(blocks, span, state_size)
-    c_blocks = c_out.reshape(blocks, span, state_size)
-    running = jnp.cumsum(log_decay, axis=1)
-    scores = jnp.einsum("zin,zjn->zij", c_blocks, b_blocks, precision=HIGHEST)
-    lower = jnp.arange(span)[:, None] >= jnp.arange(span)[None, :]
-    spread = running[:, :, None, :] - running[:, None, :, :]
-    weight = (
-        jnp.exp(jnp.where(lower[None, :, :, None], spread, -jnp.inf))
-        * scores[:, :, :, None]
-        * step_blocks[:, None, :, :]
-    )
-    within = jnp.einsum("zijh,zjhp->zihp", weight, signal_blocks, precision=HIGHEST)
-    tail = jnp.exp(running[:, -1:, :] - running) * step_blocks
-    block_state = jnp.einsum("zjh,zjhp,zjn->zhpn", tail, signal_blocks, b_blocks, precision=HIGHEST)
-    block_decay = running[:, -1, :]
-    carried = jnp.zeros((heads, head_size, state_size), jnp.float32)
-    before = jnp.zeros((heads,), jnp.float32)
-    starts = []
-    befores = []
-    for z in range(blocks):
-        starts.append(carried)
-        befores.append(before)
-        carried = jnp.exp(block_decay[z])[:, None, None] * carried + block_state[z]
-        before = before + block_decay[z]
-
-    def link(earlier, later):
-        return (earlier[0] + later[0], jnp.exp(later[0])[:, None, None] * earlier[1] + later[1])
-
-    unused, incoming = carried_in(
-        (before, carried), "seq", link, (jnp.zeros_like(before), jnp.zeros_like(carried))
-    )
-    entries = []
-    for z in range(blocks):
-        entries.append(starts[z] + jnp.exp(befores[z])[:, None, None] * incoming)
-    entry = jnp.stack(entries, 0)
-    across = jnp.exp(running)[..., None] * jnp.einsum(
-        "zin,zhpn->zihp", c_blocks, entry, precision=HIGHEST
-    )
-    scanned = within + across + skip[None, None, :, None] * signal_blocks
-    gated = scanned.reshape(tok_rows, inner_w) * jax.nn.silu(gate_z)
-    gated = (rms_rows(gated) * norm_gain).astype(jnp.bfloat16)
-    columns = gated
-    mixer_sum = jnp.dot(
-        columns,
-        lax.all_gather(w_out, "seq", axis=0, tiled=True),
-        preferred_element_type=jnp.float32,
-    )
-    mixed = (resid + mixer_sum).astype(jnp.bfloat16)
-    routed = rms_rows(mixed.astype(jnp.float32)).astype(jnp.bfloat16)
-    logits = jnp.dot(routed, w_router, preferred_element_type=jnp.float32)
-    experts = w_router.shape[1]
-    pair_ids = expert_ids.reshape(tok_rows * 2)
-    choose = (pair_ids[:, None] == jnp.arange(experts, dtype=jnp.int32)[None, :]).astype(jnp.int32)
-    picked = jnp.sum(
-        choose.reshape(tok_rows, 2, experts).astype(jnp.float32) * logits[:, None, :], axis=-1
-    )
-    first = jax.nn.sigmoid(picked[:, 0] - picked[:, 1])
-    pair_weight = jnp.stack([first, 1.0 - first], axis=1)
-    earlier_hits = jnp.cumsum(choose, axis=0) - choose
-    slot = jnp.sum(earlier_hits * choose, axis=1)
-    slot_of = slot.reshape(tok_rows, 2)
-    notes = jnp.stack(
-        [
-            expert_ids.reshape(tok_rows, 2)[:, 0].astype(jnp.float32),
-            slot_of[:, 0].astype(jnp.float32),
-            expert_ids.reshape(tok_rows, 2)[:, 1].astype(jnp.float32),
-            slot_of[:, 1].astype(jnp.float32),
-            first,
-            1.0 - first,
-        ],
-        axis=0,
-    )
-    notes = jnp.pad(notes, ((0, META - 6), (0, width - tok_rows))).astype(jnp.bfloat16)
-    block = jnp.concatenate([notes, routed], axis=0)
-    total = moe(block, mixed, w_gate, w_up, w_down)
-    return total.reshape(1, tok_rows, width)
+    return moe(block, mixed, w_gate, w_up, w_down)[None]
 
 
 def solution(mesh):

time: 298 us -> 187 us (0.63)
  waiting for transfers between devices: 99.4 us -> 0 us
  Pallas kernels: 113 us -> 171 us
  matrix products: 25.1 us -> 0 us
  blocking collectives: 17.6 us -> 0 us
  between operations: 13.5 us -> 0.07 us
  other arithmetic: 11 us -> 0 us
    all_gather x3 -> x0, waiting for transfers between devices: 98 us -> none  [the longest x1 47.4 us: local(): lax.all_gather(w_in, 'seq', axis=0, tiled=True)]
    pallas_call x0 -> x1, Pallas kernels: none -> 56.9 us  [mixer(): pl.pallas_call(mixer_kernel, out_shape=(jax.ShapeDtypeStruct((rows, width...]
    dot_general x8 -> x0, matrix products: 25.1 us -> none  [the longest x1 7.51 us: local(): jnp.einsum('zijh,zjhp->zihp', weight, signal_blocks, precision=HIGHEST)]
    all_gather x1 -> x0, blocking collectives: 17.6 us -> none  [carried_in(): gathered = jax.tree.map(lambda a: lax.all_gather(a, axis), part)]
    unnamed x41 -> x24, local copies, waits for them, and re-layouts: 4.39 us -> 11.7 us
    reshape x8 -> x2, local copies, waits for them, and re-layouts: 8.68 us -> 1.4 us  [mixer(): line = lambda v: v.reshape(1, -1)]
    reduce_sum x4 -> x0, other arithmetic: 3.89 us -> none  [the longest x2 3.71 us: rms_rows(): jnp.mean(values * values, axis=-1, keepdims=True) + EPSILON]
    mul x3 -> x0, other arithmetic: 3.44 us -> none  [the longest x1 2.13 us: local(): signal = jax.nn.silu(conv)]
  transfers between devices with their start and end apart: 4 -> 0, of which waited for: 3 -> 0; matrix products, arithmetic and copies ran while one was open for 9% -> 0% of each run, Pallas kernels for 0% -> 0%
where the time goes in v2:
time: 187 us; the launch traced here: 184 us
  Pallas kernels  171 us (91%)
  local copies, waits for them, and re-layouts  13.1 us (7%)
    pallas_call x1, Pallas kernels, moe(): pl.pallas_call(moe_kernel, out_shape=jax.ShapeDtypeStruct((rows, width),...  114 us
    pallas_call x1, Pallas kernels, mixer(): pl.pallas_call(mixer_kernel, out_shape=(jax.ShapeDtypeStruct((rows, width...  56.9 us
    unnamed x24, local copies, waits for them, and re-layouts  11.7 us

profile of v2, /device:TPU:6, one launch (start us, length us, event | category | flops | bytes accessed | tf_op | source)
XLA Modules:
  0.0 184.3 jit_solution(423755437281050982)
XLA Ops:
  0.0 0.7 reshape.17.cb_ref
  0.7 0.7 reshape.19.gain_ref
  1.4 0.8 copy.16
  2.2 1.1 copy.17.wsmall_ref
  3.3 1.0 copy.18.wr_ref
  4.2 0.0 copy-start
  4.3 1.0 copy-done
  5.2 0.0 copy-start.1
  5.3 1.0 copy-done.1
  6.2 0.0 copy-start.2
  6.2 0.9 copy-done.2
  7.1 0.0 copy-start.3
  7.1 0.7 copy-done.3
  7.9 0.0 copy-start.4
  7.9 0.7 copy-done.4
  8.5 0.0 copy-start.5
  8.5 0.7 copy-done.5
  9.2 0.0 copy-start.6
  9.2 0.7 copy-done.6
  9.8 0.0 copy-start.7
  9.8 56.9 %state_space_mixer.1 = (bf16[256,768]{1,0:T(8,128)(2,1)S(1)}, bf16[272,768]{1,0:T(8,128)(2,1)S(1)}) custom-call(bf16[256,768]{1,0:T(8,128)(2,1)S(1)} %bitcast.8, bf16[48,3072]{1,0:T(8,128)(2,1)S(1)} %copy-done.1, bf16[768,56]{1,0:T(8,128)(2,1)S(1)} %copy.17.wsmall_ref, f32[1,24]{1,0:T(1,128)S(1)} %bitcast.9, f32[1,24]{1,0:T(1,128)S(1)} %bitcast.10, ...), custom_call_target="tpu_custom_call" | custom-call | tf_op jit(solution)/shard_map/state_space_mixer/pallas_call | solution.py:765
  66.7 0.0 copy-done.7
  66.7 0.0 copy-start.8
  66.7 1.3 copy-done.8
  68.0 0.0 copy-start.9
  68.0 1.3 copy-done.9
  69.3 114.3 %expert_exchange.1 = bf16[256,768]{1,0:T(8,128)(2,1)S(1)} custom-call(bf16[272,768]{1,0:T(8,128)(2,1)S(1)} %get-tuple-element.7.blk_ref, bf16[256,768]{1,0:T(8,128)(2,1)S(1)} %get-tuple-element.8.mixed_ref, bf16[1,768,768]{2,1,0:T(8,128)(2,1)S(1)} %copy-done.7, bf16[1,768,768]{2,1,0:T(8,128)(2,1)S(1)} %copy-done.8, bf16[1,768,768]{2,1,0:T(8,128)(2,1)S(1)} %copy-done.9), custom_call_target="tpu_custom_call" | custom-call | flops 8000000000 | bytes 6000000 | tf_op jit(solution)/shard_map/expert_exchange/pallas_call | solution.py:236
  183.6 0.7 copy.20
Async XLA Ops:
  4.2 1.0 copy-start
  5.2 1.0 copy-start.1
  6.2 0.9 copy-start.2
  7.1 0.7 copy-start.3
  7.9 0.7 copy-start.4
  8.5 0.7 copy-start.5
  9.2 0.7 copy-start.6
  9.8 56.9 %copy-start.7 = (bf16[1,768,768]{2,1,0:T(8,128)(2,1)S(1)}, bf16[1,768,768]{2,1,0:T(8,128)(2,1)}, u32[]{:S(2)}) copy-start(bf16[1,768,768]{2,1,0:T(8,128)(2,1)} %wg_ref.1) | copy-start | bytes 3538948
  66.7 1.3 copy-start.8
  68.0 1.3 copy-start.9

commit v3 on v2

v3 whole, which is shorter than its diff:
```python
import jax
import jax.numpy as jnp
from jax import lax
from jax.experimental import pallas as pl
from jax.experimental.pallas import tpu as pltpu
from jax.sharding import PartitionSpec as P

Y, X = 8, 4
CAP = 48
META = 16
MESH = pl.DeviceIdType.MESH


def exp_peers():
    e = lax.axis_index("exp")
    return e // X, lax.rem(e, X)


Z = 8
HALO = 16
EPSILON = 1e-05
HIGHEST = lax.Precision.HIGHEST
F32 = jnp.float32
BF16 = jnp.bfloat16


def layer_kernel(
    tok_hbm, win_hbm, wsmall_hbm, dtb_hbm, rate_hbm, cw_hbm, cb_hbm, skip_hbm, gain_hbm, wout_hbm, wr_hbm, ids_hbm,
    wg_hbm, wu_hbm, wd_hbm, out_ref,
    tok_ref, win_ref, wsmall_ref, dtb_ref, rate_ref, cw_ref, cb_ref, skip_ref, gain_ref, wout_ref, wr_ref, ids_ref,
    wg_ref, wu_ref, wd_ref, mixed_ref,
    wi, wo, normed, ext, sig, gz, step_l, tail_l, run_l, wmat, bmat, cmat, yy, skip_l, decs, dec_out, states, state_out,
    gg, half_out, half_in, notes,
    gath, sbuf, arr, ans, ret, part_of, rs_out, rs_in, hid,
    fetch_sem,
    isend, irecv, nsend, nrecv, osend, orecv, mosend, morecv, dsend, drecv, ssend, srecv, misc_send, misc_recv,
    ysend, yrecv, xsend, xrecv, rsend, rrecv, psend, precv,
):
    rows, width = tok_ref.shape
    both = 2 * rows
    inner_w = wi.shape[1] // 2
    heads = skip_ref.shape[0] // 2
    head_size = inner_w // heads
    n_state = (wsmall_ref.shape[0] - 2 * heads) // 2
    in_rows = win_ref.shape[0]
    out_rows = wout_ref.shape[0]
    part = inner_w // 2
    seat = lax.axis_index("seq")
    z, c = seat // 2, lax.rem(seat, 2)
    y, x = exp_peers()
    pair = lax.rem(y, 2), lax.rem(x, 2)

    def device(dz=0, core=None, dy=0, dx=0):
        return {
            "seq": lax.rem(z + dz, Z) * 2 + (c if core is None else core),
            "exp": lax.rem(y + dy, Y) * X + lax.rem(x + dx, X),
        }

    sibling = device(core=1 - c)

    def remote(src, dst, send, recv, to):
        return pltpu.make_async_remote_copy(
            src_ref=src, dst_ref=dst, send_sem=send, recv_sem=recv, device_id=to, device_id_type=MESH
        )

    pairs = (
        (win_hbm, win_ref), (tok_hbm, tok_ref), (wout_hbm, wout_ref), (wsmall_hbm, wsmall_ref), (dtb_hbm, dtb_ref),
        (rate_hbm, rate_ref), (skip_hbm, skip_ref), (ids_hbm, ids_ref), (cw_hbm, cw_ref), (cb_hbm, cb_ref),
        (gain_hbm, gain_ref), (wr_hbm, wr_ref), (wg_hbm, wg_ref), (wu_hbm, wu_ref), (wd_hbm, wd_ref),
    )
    fetches = [pltpu.make_async_copy(src, dst, fetch_sem.at[n]) for n, (src, dst) in enumerate(pairs)]
    for copy in fetches:
        copy.start()

    barrier = pltpu.get_barrier_semaphore()
    peers = [sibling, device(dy=1), device(dy=Y - 1), device(dx=1), device(dx=X - 1)]
    peers += [device(dx=2)] + [device(dz=j) for j in range(1, Z)]
    for to in peers:
        pl.semaphore_signal(barrier, inc=1, device_id=to, device_id_type=MESH)
    pl.semaphore_wait(barrier, len(peers))

    def lanes(start, size):
        return pl.ds(pl.multiple_of(start, 128), size)

    def in_band(zs, h):
        return pl.ds(pl.multiple_of((2 * zs + h) * in_rows, 16), in_rows)

    def out_band(zs, h):
        return pl.ds(pl.multiple_of(lax.rem(2 * zs + h, Z) * out_rows, 16), out_rows)

    first_in = lanes(pair[0] * part, part)
    second_in = lanes(inner_w + pair[1] * part, part)
    first_out = lanes(pair[1] * part, part)

    def origin(k, side):
        return lax.rem(z + Z - k, Z) if side == 0 else lax.rem(z + k, Z)

    def landed(k, side):
        return k if side == 0 else Z - k

    def hop(k, h, side):
        band = in_band(origin(k - 1, side), h)
        to = device(dz=1 if side == 0 else Z - 1)
        return [
            remote(wi.at[band, cols], wi.at[band, cols], isend.at[side, k - 1, h], irecv.at[landed(k, side), h], to)
            for cols in (first_in, second_in)
        ]

    def in_whole(send, recv):
        return remote(wi.at[0:in_rows, 0:inner_w], wi.at[0:in_rows, 0:inner_w], send, recv, sibling)

    def hop_arrived(k, h, side):
        in_whole(isend.at[side, k - 1, h], irecv.at[landed(k, side), h]).wait_recv()

    def share(k, h, side):
        band = in_band(origin(k, side), h)
        off = landed(k, side)
        for cols, to in (
            (first_in, device(dy=1 if h == 0 else Y - 1)),
            (second_in, device(dx=1 if h == 0 else X - 1)),
        ):
            remote(wi.at[band, cols], wi.at[band, cols], nsend.at[off, h], nrecv.at[off, h], to).start()

    def out_hop(k, h, side):
        band = out_band(origin(k - 1, side), h)
        to = device(dz=1 if side == 0 else Z - 1)
        return remote(
            wo.at[band, first_out], wo.at[band, first_out], osend.at[side, k - 1, h], orecv.at[landed(k, side), h], to
        )

    def out_share(k, h, side):
        band = out_band(origin(k, side), h)
        off = landed(k, side)
        return remote(
            wo.at[band, first_out], wo.at[band, first_out], mosend.at[off, h], morecv.at[off, h],
            device(dx=1 if h == 0 else X - 1),
        )

    last = Z // 2

    def sent(k, h, side):
        return k < last or (k == last and h == side)

    def wanted(k, side):
        return origin(k, side) // last == c

    def units(k):
        return [(h, side) for h in range(2) for side in range(2) if sent(k, h, side)]

    fetches[0].wait()
    wi[in_band(z, c), 0:inner_w] = win_ref[:, lanes(2 * inner_w + c * inner_w, inner_w)]
    wi[in_band(z, c), inner_w:] = win_ref[:, lanes(c * inner_w, inner_w)]

    def to_sibling():
        return [
            remote(
                win_ref.at[:, lanes(base + (1 - c) * inner_w, inner_w)],
                wi.at[in_band(z, c), pl.ds(at, inner_w)],
                misc_send.at[0], misc_recv.at[0], sibling,
            )
            for base, at in ((2 * inner_w, 0), (0, inner_w))
        ]

    for copy in to_sibling():
        copy.start()
    for side in range(2):
        for copy in hop(1, c, side):
            copy.start()

    def out_to_sibling():
        return remote(wout_ref, wo.at[out_band(z, c)], misc_send.at[4], misc_recv.at[4], sibling)

    fetches[1].wait()
    fetches[2].wait()
    home = z // last == c

    @pl.when(home)
    def _():
        wo[out_band(z, c), :] = wout_ref[...]

    @pl.when(jnp.logical_not(home))
    def _():
        out_to_sibling().start()

    resid = tok_ref[...].astype(F32)
    scale = lax.rsqrt(jnp.mean(resid * resid, axis=-1, keepdims=True) + EPSILON)
    mine = pl.ds(pl.multiple_of(HALO + c * rows, 16), rows)
    normed[mine, :] = (resid * scale).astype(BF16)

    def rows_across():
        return remote(normed.at[mine], normed.at[mine], misc_send.at[1], misc_recv.at[1], sibling)

    rows_across().start()
    other_in = remote(
        wi.at[0:in_rows], wi.at[0:in_rows], misc_send.at[0], misc_recv.at[0], sibling
    )
    other_in.wait_recv()
    for side in range(2):
        for copy in hop(1, 1 - c, side):
            copy.start()

    rows_across().wait_recv()

    def halo():
        return remote(
            normed.at[both : both + HALO], normed.at[0:HALO], misc_send.at[2], misc_recv.at[2], device(dz=1)
        )

    @pl.when(z < Z - 1)
    def _():
        halo().start()

    @pl.when(z == 0)
    def _():
        normed[0:HALO, :] = jnp.zeros((HALO, width), BF16)

    for copy in fetches[3:8]:
        copy.wait()
    small = lax.dot_general(
        normed[HALO:, :], wsmall_ref[...], (((1,), (1,)), ((), ())), preferred_element_type=F32
    )
    bmat[...] = small[:, 0:n_state]
    cmat[...] = small[:, n_state : 2 * n_state]
    raw = small[:, 2 * n_state :] + dtb_ref[...].reshape(1, 2 * heads)
    step_all = jnp.maximum(raw, 0.0) + jnp.log1p(jnp.exp(-jnp.abs(raw)))
    decay_all = -step_all * rate_ref[...].reshape(1, 2 * heads)

    def own_heads(v):
        return jnp.where(c == 0, v[:, 0:heads], v[:, heads : 2 * heads])

    step = own_heads(step_all)
    log_decay = own_heads(decay_all)
    head_of = lax.broadcasted_iota(jnp.int32, (heads, inner_w), 1) // head_size
    spread = (head_of == lax.broadcasted_iota(jnp.int32, (heads, inner_w), 0)).astype(BF16)
    spread_f = spread.astype(F32)

    def expand(v):
        high = v.astype(BF16)
        low = (v - high.astype(F32)).astype(BF16)
        return jnp.dot(high, spread, preferred_element_type=F32) + jnp.dot(low, spread, preferred_element_type=F32)

    row_id = lax.broadcasted_iota(jnp.int32, (rows, rows), 0)
    col_id = lax.broadcasted_iota(jnp.int32, (rows, rows), 1)
    lower = (row_id >= col_id).astype(F32)
    upper = (row_id <= col_id).astype(F32)
    running, running_t, ends, scores = [], [], [], []
    for q in range(2):
        piece = log_decay[q * rows : (q + 1) * rows]
        run = jnp.dot(lower, piece, precision=HIGHEST, preferred_element_type=F32)
        running.append(run)
        running_t.append(
            lax.dot_general(piece, upper, (((0,), (0,)), ((), ())), precision=HIGHEST, preferred_element_type=F32)
        )
        end = run[rows - 1 : rows]
        ends.append(end)
        span = pl.ds(q * rows, rows)
        here = step[q * rows : (q + 1) * rows]
        step_l[span, :] = expand(here)
        tail_l[span, :] = expand(here * jnp.exp(end - run))
        run_l[span, :] = expand(jnp.exp(run))
        grid = lax.dot_general(
            cmat[span, :], bmat[span, :], (((1,), (1,)), ((), ())), precision=HIGHEST, preferred_element_type=F32
        )
        scores.append(jnp.where(row_id >= col_id, grid, 0.0))
    ends_l = [
        jnp.dot(jnp.broadcast_to(end, (8, heads)), spread_f, precision=HIGHEST, preferred_element_type=F32)
        for end in ends
    ]
    dec_out[...] = ends_l[0] + ends_l[1]
    skip_l[...] = jnp.dot(
        jnp.broadcast_to(own_heads(skip_ref[...].reshape(1, 2 * heads)), (8, heads)), spread_f,
        precision=HIGHEST, preferred_element_type=F32,
    )

    def decay_copy(j):
        return remote(dec_out, decs.at[j], dsend.at[j], drecv.at[j], device(dz=j))

    def state_copy(j):
        return remote(state_out, states.at[j], ssend.at[j], srecv.at[j], device(dz=j))

    for j in range(1, Z):

        @pl.when(z + j < Z)
        def _(j=j):
            decay_copy(j).start()

    def advance(k):
        for h, side in units(k):
            hop_arrived(k, h, side)
            if k < last and sent(k + 1, h, side):
                for copy in hop(k + 1, h, side):
                    copy.start()
            share(k, h, side)

    def weigh(q):
        for i in range(heads):
            gap = jnp.minimum(running[q][:, i : i + 1] - running_t[q][i : i + 1, :], 0.0)
            wmat[q * heads + i] = (jnp.exp(gap) * scores[q]).astype(BF16)

    @pl.when(home)
    def _():
        out_to_sibling().wait_recv()
        for h, side in units(1):
            out_hop(1, h, side).start()

    def out_advance(k):
        for h, side in units(k):

            @pl.when(wanted(k, side))
            def _(h=h, side=side):
                out_hop(k, h, side).wait_recv()
                if k < last and sent(k + 1, h, side):
                    out_hop(k + 1, h, side).start()
                out_share(k, h, side).start()

    advance(1)
    weigh(0)
    advance(2)
    out_advance(1)
    weigh(1)
    advance(3)
    out_advance(2)

    experts = wr_ref.shape[0]
    line = lax.broadcasted_iota(jnp.int32, (experts, rows), 0)
    hits = [line == ids_ref[k : k + 1, :] for k in range(2)]
    taken = (hits[0] | hits[1]).astype(F32).astype(BF16)
    before = jnp.dot(taken, (row_id < col_id).astype(F32).astype(BF16), preferred_element_type=F32)
    for k in range(2):
        notes[2 * k : 2 * k + 1, :] = jnp.sum(jnp.where(hits[k], line.astype(F32), 0.0), axis=0, keepdims=True)
        notes[2 * k + 1 : 2 * k + 2, :] = jnp.sum(jnp.where(hits[k], before, 0.0), axis=0, keepdims=True)
    notes[6:, :] = jnp.zeros((META - 6, rows), F32)

    advance(last)
    for k in range(1, last + 1):
        for h, side in units(k):
            off = landed(k, side)
            in_whole(nsend.at[off, h], nrecv.at[off, h]).wait_recv()

    out_advance(3)

    @pl.when(z > 0)
    def _():
        halo().wait_recv()

    tile = 256

    def project(i, carry):
        cols = pl.ds(pl.multiple_of(i * tile, tile), tile)
        ext[:, cols] = jnp.dot(normed[...], wi[:, cols], preferred_element_type=F32).astype(BF16).astype(F32)
        return carry

    lax.fori_loop(0, inner_w // tile, project, 0)
    for copy in fetches[8:12]:
        copy.wait()
    taps = cw_ref.shape[0]

    def convolve(i, carry):
        cols = pl.ds(pl.multiple_of(i * 128, 128), 128)
        params = lanes(c * inner_w + i * 128, 128)
        for q in range(2):
            acc = cb_ref[params].reshape(1, 128) + jnp.zeros((rows, 128), F32)
            for k in range(taps):
                acc = acc + cw_ref[k : k + 1, params] * ext[pl.ds(HALO - taps + 1 + k + q * rows, rows), cols]
            sig[pl.ds(q * rows, rows), cols] = acc * jax.nn.sigmoid(acc)
        return carry

    lax.fori_loop(0, inner_w // 128, convolve, 0)
    own_state = []
    for q in range(2):
        span = pl.ds(q * rows, rows)
        own_state.append(
            lax.dot_general(
                bmat[span, :].astype(BF16), (sig[span, :] * tail_l[span, :]).astype(BF16), (((0,), (0,)), ((), ())),
                preferred_element_type=F32,
            )
        )
    state_out[...] = (jnp.exp(ends_l[1][0:1]) * own_state[0] + own_state[1]).astype(BF16)
    for j in range(1, Z):

        @pl.when(z + j < Z)
        def _(j=j):
            state_copy(j).start()

        @pl.when(z < j)
        def _(j=j):
            states[j] = jnp.zeros_like(state_out)
            decs[j] = jnp.zeros_like(dec_out)

    out_advance(last)

    def project_gate(i, carry):
        cols = pl.ds(pl.multiple_of(i * tile, tile), tile)
        weight = wi[:, pl.ds(pl.multiple_of(inner_w + i * tile, tile), tile)]
        gz[:, cols] = jnp.dot(normed[HALO:, :], weight, preferred_element_type=F32)
        return carry

    lax.fori_loop(0, inner_w // tile, project_gate, 0)
    left_lane = lax.broadcasted_iota(jnp.int32, (rows, 128), 1) < head_size

    def within(p, carry):
        cols = pl.ds(pl.multiple_of(p * 128, 128), 128)
        skips = skip_l[0:1, cols]
        for q in range(2):
            span = pl.ds(q * rows, rows)
            fresh = (sig[span, cols] * step_l[span, cols]).astype(BF16)
            a = jnp.dot(wmat[q * heads + 2 * p], fresh, preferred_element_type=F32)
            b = jnp.dot(wmat[q * heads + 2 * p + 1], fresh, preferred_element_type=F32)
            yy[span, cols] = jnp.where(left_lane, a, b) + skips * sig[span, cols]
        return carry

    lax.fori_loop(0, inner_w // 128, within, 0)

    entry = jnp.zeros((n_state, inner_w), F32)
    lead = jnp.zeros((1, inner_w), F32)
    for j in range(1, Z):

        @pl.when(z >= j)
        def _(j=j):
            decay_copy(j).wait_recv()
            state_copy(j).wait_recv()

        entry = entry + jnp.exp(lead) * states[j].astype(F32)
        lead = lead + decs[j, 0:1]
    gain = gain_ref[lanes(c * inner_w, inner_w)].reshape(1, inner_w)
    squares = []
    for q in range(2):
        span = pl.ds(q * rows, rows)
        start = entry if q == 0 else jnp.exp(ends_l[0][0:1]) * entry + own_state[0]
        across = run_l[span, :] * jnp.dot(cmat[span, :].astype(BF16), start.astype(BF16), preferred_element_type=F32)
        gate = gz[span, :]
        gated = (yy[span, :] + across) * (gate * jax.nn.sigmoid(gate))
        squares.append(jnp.sum(gated * gated, axis=1, keepdims=True))
        gg[span, :] = (gated * gain).astype(BF16)

    for k in range(1, last + 1):
        for h, side in units(k):

            @pl.when(wanted(k, side))
            def _(k=k, h=h, side=side):
                out_share(k, h, side).wait_recv()

    theirs = pl.ds(pl.multiple_of((1 - c) * rows, 16), rows)
    ours = pl.ds(pl.multiple_of(c * rows, 16), rows)

    def leave(i, carry):
        cols = pl.ds(pl.multiple_of(i * tile, tile), tile)
        half_out[:, cols] = jnp.dot(gg[theirs, :], wo[:, cols], preferred_element_type=F32).astype(BF16)
        return carry

    lax.fori_loop(0, width // tile, leave, 0)
    wide = lax.broadcasted_iota(jnp.int32, (rows, 128), 1)
    their_square = jnp.where(c == 0, squares[1], squares[0])
    our_square = jnp.where(c == 0, squares[0], squares[1])
    high = their_square.astype(BF16).astype(F32)
    half_out[:, width:] = jnp.where(wide < 64, high, their_square - high).astype(BF16)

    def halves():
        return remote(half_out, half_in, misc_send.at[3], misc_recv.at[3], sibling)

    halves().start()

    def stay(i, carry):
        cols = pl.ds(pl.multiple_of(i * tile, tile), tile)
        yy[0:rows, cols] = jnp.dot(gg[ours, :], wo[:, cols], preferred_element_type=F32)
        return carry

    lax.fori_loop(0, width // tile, stay, 0)
    halves().wait_recv()
    extra = half_in[:, width:].astype(F32)
    total = our_square + extra[:, 0:1] + extra[:, 64:65]
    norm = lax.rsqrt(total / (2 * inner_w) + EPSILON)
    mixed = (
        tok_ref[...].astype(F32) + norm * (yy[0:rows, 0:width] + half_in[:, 0:width].astype(F32))
    ).astype(BF16)
    mixed_ref[...] = mixed
    mixed_f = mixed.astype(F32)
    routed = (mixed_f * lax.rsqrt(jnp.mean(mixed_f * mixed_f, axis=-1, keepdims=True) + EPSILON)).astype(BF16)
    gath[0, META:, :] = routed
    logits = lax.dot_general(wr_ref[...], routed, (((1,), (1,)), ((), ())), preferred_element_type=F32)
    picked = [jnp.sum(jnp.where(hit, logits, 0.0), axis=0, keepdims=True) for hit in hits]
    first = jax.nn.sigmoid(picked[0] - picked[1])
    notes[4:5, :] = first
    notes[5:6, :] = 1.0 - first
    gath[0, 0:META, 0:rows] = notes[...].astype(BF16)
    gath[0, 0:META, rows:] = jnp.zeros((META, width - rows), BF16)

    for copy in fetches[12:]:
        copy.wait()
    half = rows // 2
    slots = X * CAP
    up, down = device(dy=1), device(dy=Y - 1)
    spans = (pl.ds(0, META + half), pl.ds(META + half, half))
    bands = (pl.ds(0, half), pl.ds(half, half))

    def right(k, h):
        return remote(
            gath.at[k - 1, spans[h]], gath.at[k, spans[h]], ysend.at[0, k - 1, h], yrecv.at[k, h], up
        )

    def left(k, h):
        return remote(
            gath.at[(Y - k + 1) % Y, spans[h]], gath.at[Y - k, spans[h]], ysend.at[1, k - 1, h], yrecv.at[Y - k, h], down
        )

    def seat_of(d):
        return 0 if d == 0 else 1 if d == last else 2 * d if d < last else 2 * (Y - d) + 1

    def places(d):
        meta = gath[d, 0:META, 0:rows].astype(F32)
        at = []
        for k in range(2):
            off = meta[2 * k : 2 * k + 1, :] - (y * X).astype(F32)
            turn = off - x.astype(F32)
            turn = jnp.where(turn < 0.0, turn + X, turn)
            inside = (off >= 0.0) & (off < float(X))
            at.append(jnp.where(inside, turn * CAP + meta[2 * k + 1 : 2 * k + 2, :], -1.0))
        order = lax.broadcasted_iota(jnp.int32, (slots, 1), 0).astype(F32)
        return meta, order == at[0], order == at[1]

    def slab(n, k=0, size=slots):
        return pl.ds(n * slots + k * CAP, size)

    def sideways(n, k):
        return remote(sbuf.at[slab(n, k, CAP)], arr.at[slab(n, k, CAP)], xsend.at[n], xrecv.at[n], device(dx=k))

    def homeward(n, k):
        return remote(ans.at[slab(n, k, CAP)], ret.at[slab(n, k, CAP)], rsend.at[n], rrecv.at[n], device(dx=X - k))

    def all_sideways(n):
        span = slab(n, 1, slots - CAP)
        return remote(sbuf.at[span], arr.at[span], xsend.at[n], xrecv.at[n], up)

    def all_homeward(n):
        span = slab(n, 1, slots - CAP)
        return remote(ans.at[span], ret.at[span], rsend.at[n], rrecv.at[n], up)

    def dispatch(d):
        n = seat_of(d)
        meta, hit0, hit1 = places(d)
        pick = jnp.where(hit0 | hit1, 1.0, 0.0).astype(BF16)
        sbuf[slab(n), :] = jnp.dot(pick, gath[d, META:, :], preferred_element_type=F32).astype(BF16)
        for k in (2, 1, 3):
            sideways(n, k).start()
        arr[slab(n, 0, CAP), :] = sbuf[slab(n, 0, CAP), :]

    def expert(first_seat, count):
        for n in range(first_seat, first_seat + count):
            all_sideways(n).wait_recv()
        span = pl.ds(first_seat * slots, count * slots)
        inside = pl.ds(0, count * slots)

        def enter(i, carry):
            cols = pl.ds(pl.multiple_of(i * tile, tile), tile)
            gate = jnp.dot(arr[span, :], wg_ref[0, :, cols], preferred_element_type=F32)
            lift = jnp.dot(arr[span, :], wu_ref[0, :, cols], preferred_element_type=F32)
            hid[inside, cols] = (gate * jax.nn.sigmoid(gate) * lift).astype(BF16)
            return carry

        def close(i, carry):
            cols = pl.ds(pl.multiple_of(i * tile, tile), tile)
            ans[span, cols] = jnp.dot(hid[inside, :], wd_ref[0, :, cols], preferred_element_type=F32).astype(BF16)
            return carry

        lax.fori_loop(0, wg_ref.shape[2] // tile, enter, 0)
        lax.fori_loop(0, width // tile, close, 0)
        for n in range(first_seat, first_seat + count):
            for k in (2, 1, 3):
                homeward(n, k).start()
            ret[slab(n, 0, CAP), :] = ans[slab(n, 0, CAP), :]

    def combine(d):
        n = seat_of(d)
        all_homeward(n).wait_recv()
        meta, hit0, hit1 = places(d)
        share_of = jnp.where(hit0, meta[4:5, :], 0.0) + jnp.where(hit1, meta[5:6, :], 0.0)
        part_of[d] = lax.dot_general(
            share_of.astype(BF16), ret[slab(n), :], (((0,), (0,)), ((), ())), preferred_element_type=F32
        )

    def ring(k):
        for h in range(2):
            if sent(k, h, 0):
                right(k, h).wait_recv()
                if k < last and sent(k + 1, h, 0):
                    right(k + 1, h).start()
            if sent(k, h, 1):
                left(k, h).wait_recv()
                if k < last and sent(k + 1, h, 1):
                    left(k + 1, h).start()

    for h in range(2):
        right(1, h).start()
        left(1, h).start()
    dispatch(0)
    ring(1)
    dispatch(1)
    dispatch(Y - 1)
    ring(2)
    dispatch(2)
    dispatch(Y - 2)
    expert(seat_of(0), 1)
    ring(3)
    dispatch(3)
    dispatch(Y - 3)
    expert(seat_of(1), 2)
    combine(0)
    ring(last)
    dispatch(last)
    expert(seat_of(3), 2)
    expert(seat_of(last), 1)
    expert(seat_of(2), 2)

    def target(d, side):
        return d - 1 if side == 0 else d + 1

    def go(d, h, side):
        land = target(d, side)
        return remote(
            rs_out.at[d, bands[h]], rs_in.at[land, bands[h]], psend.at[d, h], precv.at[land, h],
            down if side == 0 else up,
        )

    def push(k, h, side):
        d = k if side == 0 else Y - k
        total = part_of[d, bands[h]]
        if k < last - 1 or (k == last - 1 and h == side):
            before_d = d + 1 if side == 0 else d - 1
            go(before_d, h, side).wait_recv()
            total = total + rs_in[d, bands[h]].astype(F32)
        rs_out[d, bands[h]] = total.astype(BF16)
        go(d, h, side).start()

    combine(3)
    push(3, 1, 0)
    combine(Y - 3)
    push(3, 0, 1)
    combine(last)
    push(last, 0, 0)
    push(last, 1, 1)
    combine(2)
    combine(Y - 2)
    push(2, 1, 0)
    push(2, 0, 1)
    combine(1)
    combine(Y - 1)
    push(3, 0, 0)
    push(3, 1, 1)
    push(1, 1, 0)
    push(1, 0, 1)
    push(2, 0, 0)
    push(2, 1, 1)
    push(1, 0, 0)
    push(1, 1, 1)
    for h in range(2):
        go(1, h, 0).wait_recv()
        go(Y - 1, h, 1).wait_recv()
        total = (
            mixed_ref[bands[h]].astype(F32) + part_of[0, bands[h]]
            + rs_in[0, bands[h]].astype(F32) + rs_in[Y, bands[h]].astype(F32)
        )
        out_ref[bands[h]] = total.astype(BF16)

    for copy in (other_in, rows_across(), halves()):
        copy.wait_send()

    @pl.when(z < Z - 1)
    def _():
        halo().wait_send()

    @pl.when(jnp.logical_not(home))
    def _():
        out_to_sibling().wait_send()

    for k in range(1, last + 1):
        for h, side in units(k):
            off = landed(k, side)
            in_whole(isend.at[side, k - 1, h], irecv.at[off, h]).wait_send()
            in_whole(nsend.at[off, h], nrecv.at[off, h]).wait_send()

            @pl.when(wanted(k - 1, side))
            def _(k=k, h=h, side=side):
                out_hop(k, h, side).wait_send()

            @pl.when(wanted(k, side))
            def _(k=k, h=h, side=side):
                out_share(k, h, side).wait_send()

    for j in range(1, Z):

        @pl.when(z + j < Z)
        def _(j=j):
            decay_copy(j).wait_send()
            state_copy(j).wait_send()
    for k in range(1, last + 1):
        for h in range(2):
            if sent(k, h, 0):
                right(k, h).wait_send()
            if sent(k, h, 1):
                left(k, h).wait_send()
    for d in range(Y):
        for h in range(2):
            if d != 0:
                go(d, h, 0).wait_send()
        all_sideways(d).wait_send()
        all_homeward(d).wait_send()


def layer(tokens, w_in, w_small, dt_bias, decay_rate, conv_w, conv_b, skip, norm_gain, w_out, w_router, ids, *experts):
    rows, width = tokens.shape
    inner_w = conv_w.shape[1] // 2
    heads = dt_bias.shape[0] // 2
    n_state = (w_small.shape[0] - 2 * heads) // 2
    both = 2 * rows
    slots = X * CAP
    hidden = experts[0].shape[2]
    dma = pltpu.SemaphoreType.DMA
    wide = pltpu.VMEM((both, inner_w), F32)
    operands = (
        tokens, w_in, w_small, dt_bias, decay_rate, conv_w, conv_b, skip, norm_gain, w_out, w_router, ids, *experts
    )
    return pl.pallas_call(
        layer_kernel,
        out_shape=jax.ShapeDtypeStruct((rows, width), BF16),
        in_specs=[pl.BlockSpec(memory_space=pltpu.HBM)] * len(operands),
        out_specs=pl.BlockSpec(memory_space=pltpu.VMEM),
        scratch_shapes=[pltpu.VMEM(v.shape, v.dtype) for v in operands] + [
            pltpu.VMEM((rows, width), BF16),
            pltpu.VMEM((width, 2 * inner_w), BF16),
            pltpu.VMEM((inner_w, width), BF16),
            pltpu.VMEM((HALO + both, width), BF16),
            pltpu.VMEM((HALO + both, inner_w), F32),
            wide, wide, wide, wide, wide,
            pltpu.VMEM((2 * heads, rows, rows), BF16),
            pltpu.VMEM((both, n_state), F32),
            pltpu.VMEM((both, n_state), F32),
            wide,
            pltpu.VMEM((8, inner_w), F32),
            pltpu.VMEM((Z, 8, inner_w), F32),
            pltpu.VMEM((8, inner_w), F32),
            pltpu.VMEM((Z, n_state, inner_w), BF16),
            pltpu.VMEM((n_state, inner_w), BF16),
            pltpu.VMEM((both, inner_w), BF16),
            pltpu.VMEM((rows, width + 128), BF16),
            pltpu.VMEM((rows, width + 128), BF16),
            pltpu.VMEM((META, rows), F32),
            pltpu.VMEM((Y, META + rows, width), BF16),
            pltpu.VMEM((Y * slots, width), BF16),
            pltpu.VMEM((Y * slots, width), BF16),
            pltpu.VMEM((Y * slots, width), BF16),
            pltpu.VMEM((Y * slots, width), BF16),
            pltpu.VMEM((Y, rows, width), F32),
            pltpu.VMEM((Y, rows, width), BF16),
            pltpu.VMEM((Y + 1, rows, width), BF16),
            pltpu.VMEM((2 * slots, hidden), BF16),
            dma((len(operands),)),
            dma((2, Z // 2, 2)), dma((Z, 2)), dma((Z, 2)), dma((Z, 2)),
            dma((2, Z // 2, 2)), dma((Z, 2)), dma((Z, 2)), dma((Z, 2)),
            dma((Z,)), dma((Z,)), dma((Z,)), dma((Z,)),
            dma((5,)), dma((5,)),
            dma((2, Y // 2, 2)), dma((Y, 2)), dma((Y,)), dma((Y,)), dma((Y,)), dma((Y,)),
            dma((Y, 2)), dma((Y + 1, 2)),
        ],
        compiler_params=pltpu.CompilerParams(
            collective_id=1, has_side_effects=True, vmem_limit_bytes=60 * 1024 * 1024
        ),
        name="mixer_and_experts",
    )(*operands)


def local(
    tokens,
    w_in,
    w_small,
    dt_bias,
    decay_rate,
    conv_w,
    conv_b,
    skip,
    norm_gain,
    w_out,
    w_router,
    expert_ids,
    w_gate,
    w_up,
    w_down,
):
    return layer(
        tokens[0], w_in, w_small.T, dt_bias, decay_rate, conv_w, conv_b, skip, norm_gain, w_out, w_router.T,
        expert_ids[0].T, w_gate, w_up, w_down,
    )[None]


def solution(mesh):
    in_specs = (
        P("exp", "seq", None),
        P("seq", None),
        P(),
        P(),
        P(),
        P(),
        P(),
        P(),
        P(),
        P("seq", None),
        P(),
        P("exp", "seq", None),
        P("exp", None, None),
        P("exp", None, None),
        P("exp", None, None),
    )
    out_specs = P("exp", "seq", None)
    return jax.shard_map(local, mesh=mesh, in_specs=in_specs, out_specs=out_specs, check_vma=False)
```

time: 187 us -> 146 us (0.78)
  Pallas kernels: 171 us -> 143 us
  local copies, waits for them, and re-layouts: 13.1 us -> 1.77 us
    pallas_call x2 -> x1, Pallas kernels: 171 us -> 143 us  [layer(): pl.pallas_call(layer_kernel, out_shape=jax.ShapeDtypeStruct((rows, width)...]
    unnamed x24 -> x1, local copies, waits for them, and re-layouts: 11.7 us -> 1.77 us
where the time goes in v3:
time: 146 us; the launch traced here: 145 us
  Pallas kernels  143 us (98%)
  local copies, waits for them, and re-layouts  1.77 us (1%)
    pallas_call x1, Pallas kernels, layer(): pl.pallas_call(layer_kernel, out_shape=jax.ShapeDtypeStruct((rows, width)...  143 us

profile of v3, /device:TPU:6, one launch (start us, length us, event | category | flops | bytes accessed | tf_op | source)
XLA Modules:
  0.0 144.8 jit_solution(15585776272096557685)
XLA Ops:
  0.0 143.0 %mixer_and_experts.1 = bf16[256,768]{1,0:T(8,128)(2,1)} custom-call(bf16[256,768]{1,0:T(8,128)(2,1)} %bitcast.8, bf16[48,3072]{1,0:T(8,128)(2,1)} %win_hbm.1, bf16[56,768]{1,0:T(8,128)(2,1)} %bitcast.9, f32[24]{0:T(128)} %dtb_hbm.1, f32[24]{0:T(128)} %rate_hbm.1, f32[4,1536]{1,0:T(4,128)} %cw_hbm.1, f32[1536]{0:T(1024)} %cb_hbm.1, f32[24]{0:T(128)} %skip_hbm.1, ...), custom_call_target="tpu_custom_call" | custom-call | tf_op jit(solution)/shard_map/mixer_and_experts/pallas_call | solution.py:722
  143.0 1.8 %copy.17 = bf16[1,256,768]{2,1,0:T(8,128)(2,1)} copy(bf16[1,256,768]{2,1,0:T(8,128)(2,1)} %bitcast.7) | data formatting | bytes 786432

commit v4 on v3

--- a/solution.py
+++ b/solution.py
@@ -31,10 +31,10 @@
     wg_ref, wu_ref, wd_ref, mixed_ref,
     wi, wo, normed, ext, sig, gz, step_l, tail_l, run_l, wmat, bmat, cmat, yy, skip_l, decs, dec_out, states, state_out,
     gg, half_out, half_in, notes,
-    gath, sbuf, arr, ans, ret, part_of, rs_out, rs_in, hid,
+    gath, memo, sbuf, arr, ans, ret, part_of, rs_out, rs_in, hid,
     fetch_sem,
     isend, irecv, nsend, nrecv, osend, orecv, mosend, morecv, dsend, drecv, ssend, srecv, misc_send, misc_recv,
-    ysend, yrecv, xsend, xrecv, rsend, rrecv, psend, precv,
+    ysend, yrecv, asend, arecv, xsend, xrecv, rsend, rrecv, psend, precv,
 ):
     rows, width = tok_ref.shape
     both = 2 * rows
@@ -476,38 +476,42 @@
     mixed_ref[...] = mixed
     mixed_f = mixed.astype(F32)
     routed = (mixed_f * lax.rsqrt(jnp.mean(mixed_f * mixed_f, axis=-1, keepdims=True) + EPSILON)).astype(BF16)
-    gath[0, META:, :] = routed
+    gath[0] = routed
     logits = lax.dot_general(wr_ref[...], routed, (((1,), (1,)), ((), ())), preferred_element_type=F32)
     picked = [jnp.sum(jnp.where(hit, logits, 0.0), axis=0, keepdims=True) for hit in hits]
     first = jax.nn.sigmoid(picked[0] - picked[1])
     notes[4:5, :] = first
     notes[5:6, :] = 1.0 - first
-    gath[0, 0:META, 0:rows] = notes[...].astype(BF16)
-    gath[0, 0:META, rows:] = jnp.zeros((META, width - rows), BF16)
+    memo[0] = notes[...].astype(BF16)
 
     for copy in fetches[12:]:
         copy.wait()
     half = rows // 2
     slots = X * CAP
     up, down = device(dy=1), device(dy=Y - 1)
-    spans = (pl.ds(0, META + half), pl.ds(META + half, half))
     bands = (pl.ds(0, half), pl.ds(half, half))
 
     def right(k, h):
         return remote(
-            gath.at[k - 1, spans[h]], gath.at[k, spans[h]], ysend.at[0, k - 1, h], yrecv.at[k, h], up
+            gath.at[k - 1, bands[h]], gath.at[k, bands[h]], ysend.at[0, k - 1, h], yrecv.at[k, h], up
         )
 
     def left(k, h):
         return remote(
-            gath.at[(Y - k + 1) % Y, spans[h]], gath.at[Y - k, spans[h]], ysend.at[1, k - 1, h], yrecv.at[Y - k, h], down
-        )
+            gath.at[(Y - k + 1) % Y, bands[h]], gath.at[Y - k, bands[h]], ysend.at[1, k - 1, h], yrecv.at[Y - k, h], down
+        )
+
+    def notes_right(k):
+        return remote(memo.at[k - 1], memo.at[k], asend.at[0, k - 1], arecv.at[k], up)
+
+    def notes_left(k):
+        return remote(memo.at[(Y - k + 1) % Y], memo.at[Y - k], asend.at[1, k - 1], arecv.at[Y - k], down)
 
     def seat_of(d):
         return 0 if d == 0 else 1 if d == last else 2 * d if d < last else 2 * (Y - d) + 1
 
     def places(d):
-        meta = gath[d, 0:META, 0:rows].astype(F32)
+        meta = memo[d].astype(F32)
         at = []
         for k in range(2):
             off = meta[2 * k : 2 * k + 1, :] - (y * X).astype(F32)
@@ -539,7 +543,7 @@
         n = seat_of(d)
         meta, hit0, hit1 = places(d)
         pick = jnp.where(hit0 | hit1, 1.0, 0.0).astype(BF16)
-        sbuf[slab(n), :] = jnp.dot(pick, gath[d, META:, :], preferred_element_type=F32).astype(BF16)
+        sbuf[slab(n), :] = jnp.dot(pick, gath[d], preferred_element_type=F32).astype(BF16)
         for k in (2, 1, 3):
             sideways(n, k).start()
         arr[slab(n, 0, CAP), :] = sbuf[slab(n, 0, CAP), :]
@@ -578,38 +582,53 @@
             share_of.astype(BF16), ret[slab(n), :], (((0,), (0,)), ((), ())), preferred_element_type=F32
         )
 
-    def ring(k):
-        for h in range(2):
-            if sent(k, h, 0):
-                right(k, h).wait_recv()
-                if k < last and sent(k + 1, h, 0):
-                    right(k + 1, h).start()
-            if sent(k, h, 1):
-                left(k, h).wait_recv()
-                if k < last and sent(k + 1, h, 1):
-                    left(k + 1, h).start()
+    def ring(k, h):
+        if sent(k, h, 0):
+            right(k, h).wait_recv()
+            if k < last and sent(k + 1, h, 0):
+                right(k + 1, h).start()
+        if sent(k, h, 1):
+            left(k, h).wait_recv()
+            if k < last and sent(k + 1, h, 1):
+                left(k + 1, h).start()
+        if h == 0:
+            notes_right(k).wait_recv()
+            if k < last:
+                notes_left(k).wait_recv()
+                notes_right(k + 1).start()
+            if k < last - 1:
+                notes_left(k + 1).start()
 
     for h in range(2):
         right(1, h).start()
         left(1, h).start()
+        if h == 0:
+            notes_right(1).start()
+            notes_left(1).start()
     dispatch(0)
-    ring(1)
+    ring(1, 0)
+    ring(1, 1)
     dispatch(1)
     dispatch(Y - 1)
-    ring(2)
+    expert(seat_of(0), 1)
+    ring(2, 0)
+    expert(seat_of(1), 2)
+    ring(2, 1)
     dispatch(2)
     dispatch(Y - 2)
-    expert(seat_of(0), 1)
-    ring(3)
+    combine(0)
+    ring(3, 0)
+    expert(seat_of(2), 2)
+    ring(3, 1)
     dispatch(3)
     dispatch(Y - 3)
-    expert(seat_of(1), 2)
-    combine(0)
-    ring(last)
+    combine(1)
+    combine(Y - 1)
+    ring(last, 0)
+    ring(last, 1)
     dispatch(last)
     expert(seat_of(3), 2)
     expert(seat_of(last), 1)
-    expert(seat_of(2), 2)
 
     def target(d, side):
         return d - 1 if side == 0 else d + 1
@@ -631,6 +650,8 @@
         rs_out[d, bands[h]] = total.astype(BF16)
         go(d, h, side).start()
 
+    combine(2)
+    combine(Y - 2)
     combine(3)
     push(3, 1, 0)
     combine(Y - 3)
@@ -638,12 +659,8 @@
     combine(last)
     push(last, 0, 0)
     push(last, 1, 1)
-    combine(2)
-    combine(Y - 2)
     push(2, 1, 0)
     push(2, 0, 1)
-    combine(1)
-    combine(Y - 1)
     push(3, 0, 0)
     push(3, 1, 1)
     push(1, 1, 0)
@@ -693,6 +710,9 @@
             decay_copy(j).wait_send()
             state_copy(j).wait_send()
     for k in range(1, last + 1):
+        notes_right(k).wait_send()
+        if k < last:
+            notes_left(k).wait_send()
         for h in range(2):
             if sent(k, h, 0):
                 right(k, h).wait_send()
@@ -744,7 +764,8 @@
             pltpu.VMEM((rows, width + 128), BF16),
             pltpu.VMEM((rows, width + 128), BF16),
             pltpu.VMEM((META, rows), F32),
-            pltpu.VMEM((Y, META + rows, width), BF16),
+            pltpu.VMEM((Y, rows, width), BF16),
+            pltpu.VMEM((Y, META, rows), BF16),
             pltpu.VMEM((Y * slots, width), BF16),
             pltpu.VMEM((Y * slots, width), BF16),
             pltpu.VMEM((Y * slots, width), BF16),
@@ -758,7 +779,7 @@
             dma((2, Z // 2, 2)), dma((Z, 2)), dma((Z, 2)), dma((Z, 2)),
             dma((Z,)), dma((Z,)), dma((Z,)), dma((Z,)),
             dma((5,)), dma((5,)),
-            dma((2, Y // 2, 2)), dma((Y, 2)), dma((Y,)), dma((Y,)), dma((Y,)), dma((Y,)),
+            dma((2, Y // 2, 2)), dma((Y, 2)), dma((2, Y // 2)), dma((Y,)), dma((Y,)), dma((Y,)), dma((Y,)), dma((Y,)),
             dma((Y, 2)), dma((Y + 1, 2)),
         ],
         compiler_params=pltpu.CompilerParams(

time: 146 us -> 156 us (1.068)
  Pallas kernels: 143 us -> 152 us
    pallas_call x1, Pallas kernels: 143 us -> 152 us  [layer(): pl.pallas_call(layer_kernel, out_shape=jax.ShapeDtypeStruct((rows, width)...]
where the time goes in v4:
time: 156 us; the launch traced here: 153 us
  Pallas kernels  152 us (97%)
  local copies, waits for them, and re-layouts  1.77 us (1%)
    pallas_call x1, Pallas kernels, layer(): pl.pallas_call(layer_kernel, out_shape=jax.ShapeDtypeStruct((rows, width)...  152 us

profile of v4, /device:TPU:6, one launch (start us, length us, event | category | flops | bytes accessed | tf_op | source)
XLA Modules:
  0.0 153.4 jit_solution(7381218020789163843)
XLA Ops:
  0.0 151.6 %mixer_and_experts.1 = bf16[256,768]{1,0:T(8,128)(2,1)} custom-call(bf16[256,768]{1,0:T(8,128)(2,1)} %bitcast.8, bf16[48,3072]{1,0:T(8,128)(2,1)} %win_hbm.1, bf16[56,768]{1,0:T(8,128)(2,1)} %bitcast.9, f32[24]{0:T(128)} %dtb_hbm.1, f32[24]{0:T(128)} %rate_hbm.1, f32[4,1536]{1,0:T(4,128)} %cw_hbm.1, f32[1536]{0:T(1024)} %cb_hbm.1, f32[24]{0:T(128)} %skip_hbm.1, ...), custom_call_target="tpu_custom_call" | custom-call | tf_op jit(solution)/shard_map/mixer_and_experts/pallas_call | solution.py:742
  151.6 1.8 %copy.17 = bf16[1,256,768]{2,1,0:T(8,128)(2,1)} copy(bf16[1,256,768]{2,1,0:T(8,128)(2,1)} %bitcast.7) | data formatting | bytes 786432

commit v5 on v4

--- a/solution.py
+++ b/solution.py
@@ -230,6 +230,31 @@
 
     step = own_heads(step_all)
     log_decay = own_heads(decay_all)
+    def advance(k):
+        for h, side in units(k):
+            hop_arrived(k, h, side)
+            if k < last and sent(k + 1, h, side):
+                for copy in hop(k + 1, h, side):
+                    copy.start()
+            share(k, h, side)
+
+    @pl.when(home)
+    def _():
+        out_to_sibling().wait_recv()
+        for h, side in units(1):
+            out_hop(1, h, side).start()
+
+    def out_advance(k):
+        for h, side in units(k):
+
+            @pl.when(wanted(k, side))
+            def _(h=h, side=side):
+                out_hop(k, h, side).wait_recv()
+                if k < last and sent(k + 1, h, side):
+                    out_hop(k + 1, h, side).start()
+                out_share(k, h, side).start()
+
+    advance(1)
     head_of = lax.broadcasted_iota(jnp.int32, (heads, inner_w), 1) // head_size
     spread = (head_of == lax.broadcasted_iota(jnp.int32, (heads, inner_w), 0)).astype(BF16)
     spread_f = spread.astype(F32)
@@ -284,42 +309,17 @@
         def _(j=j):
             decay_copy(j).start()
 
-    def advance(k):
-        for h, side in units(k):
-            hop_arrived(k, h, side)
-            if k < last and sent(k + 1, h, side):
-                for copy in hop(k + 1, h, side):
-                    copy.start()
-            share(k, h, side)
-
     def weigh(q):
         for i in range(heads):
             gap = jnp.minimum(running[q][:, i : i + 1] - running_t[q][i : i + 1, :], 0.0)
             wmat[q * heads + i] = (jnp.exp(gap) * scores[q]).astype(BF16)
 
-    @pl.when(home)
-    def _():
-        out_to_sibling().wait_recv()
-        for h, side in units(1):
-            out_hop(1, h, side).start()
-
-    def out_advance(k):
-        for h, side in units(k):
-
-            @pl.when(wanted(k, side))
-            def _(h=h, side=side):
-                out_hop(k, h, side).wait_recv()
-                if k < last and sent(k + 1, h, side):
-                    out_hop(k + 1, h, side).start()
-                out_share(k, h, side).start()
-
-    advance(1)
-    weigh(0)
     advance(2)
     out_advance(1)
-    weigh(1)
+    weigh(0)
     advance(3)
     out_advance(2)
+    weigh(1)
 
     experts = wr_ref.shape[0]
     line = lax.broadcasted_iota(jnp.int32, (experts, rows), 0)
@@ -548,7 +548,7 @@
             sideways(n, k).start()
         arr[slab(n, 0, CAP), :] = sbuf[slab(n, 0, CAP), :]
 
-    def expert(first_seat, count):
+    def expert(first_seat, count, answer=True):
         for n in range(first_seat, first_seat + count):
             all_sideways(n).wait_recv()
         span = pl.ds(first_seat * slots, count * slots)
@@ -568,6 +568,10 @@
 
         lax.fori_loop(0, wg_ref.shape[2] // tile, enter, 0)
         lax.fori_loop(0, width // tile, close, 0)
+        if answer:
+            reply(first_seat, count)
+
+    def reply(first_seat, count):
         for n in range(first_seat, first_seat + count):
             for k in (2, 1, 3):
                 homeward(n, k).start()
@@ -610,23 +614,20 @@
     ring(1, 1)
     dispatch(1)
     dispatch(Y - 1)
-    expert(seat_of(0), 1)
     ring(2, 0)
-    expert(seat_of(1), 2)
     ring(2, 1)
     dispatch(2)
     dispatch(Y - 2)
-    combine(0)
+    expert(seat_of(0), 1)
     ring(3, 0)
-    expert(seat_of(2), 2)
     ring(3, 1)
     dispatch(3)
     dispatch(Y - 3)
-    combine(1)
-    combine(Y - 1)
+    expert(seat_of(1), 2, False)
     ring(last, 0)
     ring(last, 1)
     dispatch(last)
+    expert(seat_of(2), 2, False)
     expert(seat_of(3), 2)
     expert(seat_of(last), 1)
 
@@ -650,8 +651,7 @@
         rs_out[d, bands[h]] = total.astype(BF16)
         go(d, h, side).start()
 
-    combine(2)
-    combine(Y - 2)
+    combine(0)
     combine(3)
     push(3, 1, 0)
     combine(Y - 3)
@@ -659,14 +659,20 @@
     combine(last)
     push(last, 0, 0)
     push(last, 1, 1)
-    push(2, 1, 0)
-    push(2, 0, 1)
+    reply(seat_of(2), 2)
+    reply(seat_of(1), 2)
     push(3, 0, 0)
     push(3, 1, 1)
+    combine(2)
+    push(2, 1, 0)
+    combine(Y - 2)
+    push(2, 0, 1)
+    combine(1)
+    combine(Y - 1)
+    push(2, 0, 0)
+    push(2, 1, 1)
     push(1, 1, 0)
     push(1, 0, 1)
-    push(2, 0, 0)
-    push(2, 1, 1)
     push(1, 0, 0)
     push(1, 1, 1)
     for h in range(2):

time: 156 us -> 135 us (0.87)
  Pallas kernels: 152 us -> 132 us
    pallas_call x1, Pallas kernels: 152 us -> 132 us  [layer(): pl.pallas_call(layer_kernel, out_shape=jax.ShapeDtypeStruct((rows, width)...]
where the time goes in v5:
time: 135 us; the launch traced here: 133 us
  Pallas kernels  132 us (98%)
  local copies, waits for them, and re-layouts  1.77 us (1%)
    pallas_call x1, Pallas kernels, layer(): pl.pallas_call(layer_kernel, out_shape=jax.ShapeDtypeStruct((rows, width)...  132 us

profile of v5, /device:TPU:6, one launch (start us, length us, event | category | flops | bytes accessed | tf_op | source)
XLA Modules:
  0.0 133.4 jit_solution(5200909527291807699)
XLA Ops:
  0.0 131.6 %mixer_and_experts.1 = bf16[256,768]{1,0:T(8,128)(2,1)} custom-call(bf16[256,768]{1,0:T(8,128)(2,1)} %bitcast.8, bf16[48,3072]{1,0:T(8,128)(2,1)} %win_hbm.1, bf16[56,768]{1,0:T(8,128)(2,1)} %bitcast.9, f32[24]{0:T(128)} %dtb_hbm.1, f32[24]{0:T(128)} %rate_hbm.1, f32[4,1536]{1,0:T(4,128)} %cw_hbm.1, f32[1536]{0:T(1024)} %cb_hbm.1, f32[24]{0:T(128)} %skip_hbm.1, ...), custom_call_target="tpu_custom_call" | custom-call | tf_op jit(solution)/shard_map/mixer_and_experts/pallas_call | solution.py:748
  131.7 1.8 %copy.17 = bf16[1,256,768]{2,1,0:T(8,128)(2,1)} copy(bf16[1,256,768]{2,1,0:T(8,128)(2,1)} %bitcast.7) | data formatting | bytes 786432

commit v6 on v5

--- a/solution.py
+++ b/solution.py
@@ -77,7 +77,6 @@
     peers += [device(dx=2)] + [device(dz=j) for j in range(1, Z)]
     for to in peers:
         pl.semaphore_signal(barrier, inc=1, device_id=to, device_id_type=MESH)
-    pl.semaphore_wait(barrier, len(peers))
 
     def lanes(start, size):
         return pl.ds(pl.multiple_of(start, 128), size)
@@ -161,18 +160,29 @@
             for base, at in ((2 * inner_w, 0), (0, inner_w))
         ]
 
+    def out_to_sibling():
+        return remote(wout_ref, wo.at[out_band(z, c)], misc_send.at[4], misc_recv.at[4], sibling)
+
+    fetches[1].wait()
+    fetches[2].wait()
+    home = z // last == c
+
+    resid = tok_ref[...].astype(F32)
+    scale = lax.rsqrt(jnp.mean(resid * resid, axis=-1, keepdims=True) + EPSILON)
+    mine = pl.ds(pl.multiple_of(HALO + c * rows, 16), rows)
+    normed[mine, :] = (resid * scale).astype(BF16)
+
+    pl.semaphore_wait(barrier, len(peers))
     for copy in to_sibling():
         copy.start()
     for side in range(2):
         for copy in hop(1, c, side):
             copy.start()
 
-    def out_to_sibling():
-        return remote(wout_ref, wo.at[out_band(z, c)], misc_send.at[4], misc_recv.at[4], sibling)
-
-    fetches[1].wait()
-    fetches[2].wait()
-    home = z // last == c
+    def rows_across():
+        return remote(normed.at[mine], normed.at[mine], misc_send.at[1], misc_recv.at[1], sibling)
+
+    rows_across().start()
 
     @pl.when(home)
     def _():
@@ -182,15 +192,6 @@
     def _():
         out_to_sibling().start()
 
-    resid = tok_ref[...].astype(F32)
-    scale = lax.rsqrt(jnp.mean(resid * resid, axis=-1, keepdims=True) + EPSILON)
-    mine = pl.ds(pl.multiple_of(HALO + c * rows, 16), rows)
-    normed[mine, :] = (resid * scale).astype(BF16)
-
-    def rows_across():
-        return remote(normed.at[mine], normed.at[mine], misc_send.at[1], misc_recv.at[1], sibling)
-
-    rows_across().start()
     other_in = remote(
         wi.at[0:in_rows], wi.at[0:in_rows], misc_send.at[0], misc_recv.at[0], sibling
     )
@@ -236,6 +237,7 @@
             if k < last and sent(k + 1, h, side):
                 for copy in hop(k + 1, h, side):
                     copy.start()
+        for h, side in units(k):
             share(k, h, side)
 
     @pl.when(home)
@@ -476,30 +478,32 @@
     mixed_ref[...] = mixed
     mixed_f = mixed.astype(F32)
     routed = (mixed_f * lax.rsqrt(jnp.mean(mixed_f * mixed_f, axis=-1, keepdims=True) + EPSILON)).astype(BF16)
+    half = rows // 2
+    broad = 384
+    slots = X * CAP
+    up, down = device(dy=1), device(dy=Y - 1)
+    bands = (pl.ds(0, half), pl.ds(half, half))
+
+    def right(k, h):
+        return remote(
+            gath.at[k - 1, bands[h]], gath.at[k, bands[h]], ysend.at[0, k - 1, h], yrecv.at[k, h], up
+        )
+
+    def left(k, h):
+        return remote(
+            gath.at[(Y - k + 1) % Y, bands[h]], gath.at[Y - k, bands[h]], ysend.at[1, k - 1, h], yrecv.at[Y - k, h], down
+        )
+
     gath[0] = routed
+    for h in range(2):
+        right(1, h).start()
+        left(1, h).start()
     logits = lax.dot_general(wr_ref[...], routed, (((1,), (1,)), ((), ())), preferred_element_type=F32)
     picked = [jnp.sum(jnp.where(hit, logits, 0.0), axis=0, keepdims=True) for hit in hits]
     first = jax.nn.sigmoid(picked[0] - picked[1])
     notes[4:5, :] = first
     notes[5:6, :] = 1.0 - first
     memo[0] = notes[...].astype(BF16)
-
-    for copy in fetches[12:]:
-        copy.wait()
-    half = rows // 2
-    slots = X * CAP
-    up, down = device(dy=1), device(dy=Y - 1)
-    bands = (pl.ds(0, half), pl.ds(half, half))
-
-    def right(k, h):
-        return remote(
-            gath.at[k - 1, bands[h]], gath.at[k, bands[h]], ysend.at[0, k - 1, h], yrecv.at[k, h], up
-        )
-
-    def left(k, h):
-        return remote(
-            gath.at[(Y - k + 1) % Y, bands[h]], gath.at[Y - k, bands[h]], ysend.at[1, k - 1, h], yrecv.at[Y - k, h], down
-        )
 
     def notes_right(k):
         return remote(memo.at[k - 1], memo.at[k], asend.at[0, k - 1], arecv.at[k], up)
@@ -555,19 +559,19 @@
         inside = pl.ds(0, count * slots)
 
         def enter(i, carry):
-            cols = pl.ds(pl.multiple_of(i * tile, tile), tile)
+            cols = pl.ds(pl.multiple_of(i * broad, broad), broad)
             gate = jnp.dot(arr[span, :], wg_ref[0, :, cols], preferred_element_type=F32)
             lift = jnp.dot(arr[span, :], wu_ref[0, :, cols], preferred_element_type=F32)
             hid[inside, cols] = (gate * jax.nn.sigmoid(gate) * lift).astype(BF16)
             return carry
 
         def close(i, carry):
-            cols = pl.ds(pl.multiple_of(i * tile, tile), tile)
+            cols = pl.ds(pl.multiple_of(i * broad, broad), broad)
             ans[span, cols] = jnp.dot(hid[inside, :], wd_ref[0, :, cols], preferred_element_type=F32).astype(BF16)
             return carry
 
-        lax.fori_loop(0, wg_ref.shape[2] // tile, enter, 0)
-        lax.fori_loop(0, width // tile, close, 0)
+        lax.fori_loop(0, wg_ref.shape[2] // broad, enter, 0)
+        lax.fori_loop(0, width // broad, close, 0)
         if answer:
             reply(first_seat, count)
 
@@ -603,12 +607,10 @@
             if k < last - 1:
                 notes_left(k + 1).start()
 
-    for h in range(2):
-        right(1, h).start()
-        left(1, h).start()
-        if h == 0:
-            notes_right(1).start()
-            notes_left(1).start()
+    notes_right(1).start()
+    notes_left(1).start()
+    for copy in fetches[12:]:
+        copy.wait()
     dispatch(0)
     ring(1, 0)
     ring(1, 1)
@@ -618,7 +620,7 @@
     ring(2, 1)
     dispatch(2)
     dispatch(Y - 2)
-    expert(seat_of(0), 1)
+    expert(seat_of(0), 1, False)
     ring(3, 0)
     ring(3, 1)
     dispatch(3)
@@ -651,7 +653,6 @@
         rs_out[d, bands[h]] = total.astype(BF16)
         go(d, h, side).start()
 
-    combine(0)
     combine(3)
     push(3, 1, 0)
     combine(Y - 3)
@@ -661,6 +662,7 @@
     push(last, 1, 1)
     reply(seat_of(2), 2)
     reply(seat_of(1), 2)
+    reply(seat_of(0), 1)
     push(3, 0, 0)
     push(3, 1, 1)
     combine(2)
@@ -675,6 +677,7 @@
     push(1, 0, 1)
     push(1, 0, 0)
     push(1, 1, 1)
+    combine(0)
     for h in range(2):
         go(1, h, 0).wait_recv()
         go(Y - 1, h, 1).wait_recv()

time: 135 us -> 136 us (level)
  the two profiles are of different devices: /device:TPU:6 before, /device:TPU:256 now
where the time goes in v6:
time: 136 us
  Pallas kernels  134 us (99%)
  local copies, waits for them, and re-layouts  1.77 us (1%)
    pallas_call x1, Pallas kernels, layer(): pl.pallas_call(layer_kernel, out_shape=jax.ShapeDtypeStruct((rows, width)...  134 us

profile of v6, /device:TPU:256, one launch (start us, length us, event | category | flops | bytes accessed | tf_op | source)
XLA Modules:
  0.0 135.7 jit_solution(6189186080569691104)
XLA Ops:
  0.0 133.9 %mixer_and_experts.1 = bf16[256,768]{1,0:T(8,128)(2,1)} custom-call(bf16[256,768]{1,0:T(8,128)(2,1)} %bitcast.8, bf16[48,3072]{1,0:T(8,128)(2,1)} %win_hbm.1, bf16[56,768]{1,0:T(8,128)(2,1)} %bitcast.9, f32[24]{0:T(128)} %dtb_hbm.1, f32[24]{0:T(128)} %rate_hbm.1, f32[4,1536]{1,0:T(4,128)} %cw_hbm.1, f32[1536]{0:T(1024)} %cb_hbm.1, f32[24]{0:T(128)} %skip_hbm.1, ...), custom_call_target="tpu_custom_call" | custom-call | tf_op jit(solution)/shard_map/mixer_and_experts/pallas_call | solution.py:751
  133.9 1.8 %copy.17 = bf16[1,256,768]{2,1,0:T(8,128)(2,1)} copy(bf16[1,256,768]{2,1,0:T(8,128)(2,1)} %bitcast.7) | data formatting | bytes 786432
